TPU v7x, 256 devices: a whole 4x4x8 slice. The times are simulated.
256 devices in a mesh: row: 8 (over z), col: 32 (over x, y, core).
Axes of the slice: x: 4, y: 4, z: 8, core: 2. Of those that a mesh axis runs over, the one named last changes fastest.
Arguments:
- rhs: float32 [4, 128, 1024, 64], P(None, 'row', 'col'), may hold values from -6 to 6
- dinv: float32 [4, 1024, 128, 128], P(None, 'col', 'row'), as said below
- panels: float32 [4, 8, 1024, 128, 128], P(None, None, 'col', 'row'), may hold values from -0.25 to 0.25
- pattern: int32 [4, 7, 1024], P(None, None, 'col'), may hold values 0 or 1
- parent_owner: int32 [3, 1024, 1], P(None, 'col'), may hold values from 0 to 31; in each aligned block of 32 rows (0 to 31, 32 to 63, ..., all dimensions but the last counted through in order) at most 2 rows name the same one
- parent_local: int32 [3, 1024], P(None, 'col'), may hold values from 0 to 31
- ancestor_solution: float32 [128, 1024, 8, 64], P('row', 'col'), may hold values from -6 to 6
Outputs:
- solution: float32 [4, 128, 1024, 64], P(None, 'row', 'col')
- boundary_update: float32 [128, 1024, 8, 64], P('row', 'col')
Inputs may be any that keep to these rules, and one draw needn't show every extreme that they name: `dinv`: each block is lower triangular with a positive diagonal. `parent_owner`: among the supernodes of one level on one index of col, at most 2 have their parent on the same index of col, and some index of col reaches 2.
All inputs are finite; a program needn't handle non-finite values. No bound on the sum of `pattern` on one device may be relied on, other than what follows from the above.
Results may differ from a plain program's by a relative error of at most 0.0001.
Values sent between devices are 32-bit elements; how exact they have to be, the bound alone decides.
A program may use at most 128 MiB of HBM per device.

v0:
```python
import jax
import jax.numpy as jnp
from jax import lax
from jax.sharding import PartitionSpec as P

RHS_COLS = 64
ANCESTORS = 8
LEVELS = 4
SUPER_COL = 32


def slot_tables(owners, local_ids, col_count, capacity):
    slot_total = col_count * capacity
    one_hot = (owners[:, None] == jnp.arange(col_count, dtype=jnp.int32)[None, :]).astype(jnp.int32)
    earlier = jnp.cumsum(one_hot, axis=0) - one_hot
    slot_index = jnp.sum(earlier * one_hot, axis=1)
    position = owners * capacity + slot_index
    matches = jnp.arange(slot_total, dtype=jnp.int32)[:, None] == position[None, :]
    sender = matches.astype(jnp.float32)
    parent_ids = jnp.sum(jnp.where(matches, local_ids[None, :] + 1, 0), axis=1)
    return (sender, parent_ids)


def spread(table, values):
    return jnp.einsum("pk,ikf->pif", table, values, precision=lax.Precision.HIGHEST)


def collect(table, values):
    return jnp.einsum("pk,pif->ikf", table, values, precision=lax.Precision.HIGHEST)


def per_device(rhs, dinv, panels, pattern, parent_owner, parent_local, ancestor_solution):
    highest = lax.Precision.HIGHEST
    row_part = rhs.shape[1]
    col_count = lax.axis_size("col")
    capacity = 2 * SUPER_COL // col_count
    width = ANCESTORS * RHS_COLS
    upper_width = width - RHS_COLS
    block_masks = [
        jnp.concatenate(
            [jnp.ones((SUPER_COL, 1), jnp.float32), pattern[height].T.astype(jnp.float32)], axis=1
        )
        for height in range(LEVELS)
    ]
    child_sum = jnp.zeros((row_part, SUPER_COL, RHS_COLS), jnp.float32)
    carried = jnp.zeros((row_part, SUPER_COL, width), jnp.float32)
    solved = []
    senders = []
    receivers = []
    outgoing = carried
    for height in range(LEVELS):
        residual = rhs[height] - child_sum
        gathered = lax.all_gather(residual, "row", axis=0, tiled=True)
        solved_rows = jnp.einsum("kib,bkr->ikr", dinv[height], gathered, precision=highest)
        solved.append(solved_rows)
        solved_all = lax.all_gather(solved_rows, "row", axis=0, tiled=True)
        product = jnp.einsum("dkib,bkr->ikdr", panels[height], solved_all, precision=highest)
        outgoing = (product * block_masks[height][None, :, :, None]).reshape(
            row_part, SUPER_COL, width
        ) + carried
        if height < LEVELS - 1:
            sender, parent_ids = slot_tables(
                parent_owner[height, :, 0], parent_local[height], col_count, capacity
            )
            packed = spread(sender, outgoing).reshape(col_count, capacity, row_part, width)
            arrived, arrived_ids = (
                lax.all_to_all(packed, "col", split_axis=0, concat_axis=0, tiled=True),
                lax.all_to_all(
                    parent_ids.reshape(col_count, capacity),
                    "col",
                    split_axis=0,
                    concat_axis=0,
                    tiled=True,
                ),
            )
            receiver = (
                arrived_ids.reshape(-1)[:, None]
                == jnp.arange(1, SUPER_COL + 1, dtype=jnp.int32)[None, :]
            ).astype(jnp.float32)
            summed = collect(receiver, arrived.reshape(col_count * capacity, row_part, width))
            child_sum = summed[:, :, :RHS_COLS]
            carried = jnp.concatenate([summed[:, :, RHS_COLS:], jnp.zeros_like(child_sum)], axis=2)
            senders.append(sender)
            receivers.append(receiver)
    boundary_update = outgoing.reshape(row_part, SUPER_COL, ANCESTORS, RHS_COLS)
    ancestry = ancestor_solution.reshape(row_part, SUPER_COL, width)
    results = [None] * LEVELS
    for height in reversed(range(LEVELS)):
        if height < LEVELS - 1:
            above = results[height + 1]
            receiver = receivers[height]
            downward = jnp.concatenate([above, ancestry[:, :, :upper_width]], axis=2)
            returned = lax.all_to_all(
                spread(receiver, downward).reshape(col_count, capacity, row_part, width),
                "col",
                split_axis=0,
                concat_axis=0,
                tiled=True,
            )
            joined = returned.reshape(col_count * capacity, row_part, width)
            ancestry = collect(senders[height], joined)
        masked = (
            ancestry.reshape(row_part, SUPER_COL, ANCESTORS, RHS_COLS)
            * block_masks[height][None, :, :, None]
        )
        piece = panels[height]
        reduced = solved[height] - lax.psum_scatter(
            jnp.einsum("dkib,ikdr->bkr", piece, masked, precision=highest),
            "row",
            scatter_dimension=0,
            tiled=True,
        )
        diagonal_piece = dinv[height]
        results[height] = lax.psum_scatter(
            jnp.einsum("kic,ikr->ckr", diagonal_piece, reduced, precision=highest),
            "row",
            scatter_dimension=0,
            tiled=True,
        )
    return (jnp.stack(results), boundary_update)


def solution(mesh):
    placed = (
        P(None, "row", "col", None),
        P(None, "col", "row", None),
        P(None, None, "col", "row", None),
        P(None, None, "col"),
        P(None, "col", None),
        P(None, "col"),
        P("row", "col", None, None),
    )
    return jax.shard_map(
        per_device,
        mesh=mesh,
        in_specs=placed,
        out_specs=(P(None, "row", "col", None), P("row", "col", None, None)),
        check_vma=False,
    )
```

profile of v0, /device:TPU:2, one launch (start us, length us, event | category | flops | bytes accessed | tf_op | source)
XLA Modules:
  0.0 1074.1 jit_solution(7026289608718906197)
XLA Ops:
  10.1 44.4 %all-gather.24.cloned.1.call-done = f32[1,128,32,64]{3,2,0,1:T(8,128)} async-done(((f32[1,16,32,64]{3,2,0,1:T(8,128)}), f32[1,128,32,64]{3,2,0,1:T(8,128)}) %all-gather.24.cloned.1.call-update) | async-done | bytes 1048592 | tf_op jit(solution)/shard_map/all_gather | solution.py:53
  61.8 7.4 all-to-all-start
  69.4 9.3 slice_bitcast_fusion.4
  78.7 21.6 %all-gather.10.cloned.1.call-done = f32[128,32,64]{2,0,1:T(8,128)} async-done(((f32[16,32,64]{2,0,1:T(8,128)}), f32[128,32,64]{2,0,1:T(8,128)}) %all-gather.10.cloned.1.call-update) | async-done | bytes 1048592 | tf_op jit(solution)/shard_map/all_gather | solution.py:56
  112.2 7.5 all-to-all-start.1
  121.2 24.4 %all-to-all-done.1 = f32[32,2,16,512]{3,2,1,0:T(8,128)} async-done(((f32[32,2,16,512]{3,2,1,0:T(8,128)}), f32[32,2,16,512]{3,2,1,0:T(8,128)}, u32[]{:S(2)}, u32[]{:S(2)}) %all-to-all-start.1) | async-done | bytes 2097184 | tf_op jit(solution)/shard_map/all_to_all | solution.py:67
  151.0 38.6 %all-gather.12.cloned.1.call-done = f32[128,32,64]{2,1,0:T(8,128)} async-done(((f32[16,32,64]{2,1,0:T(8,128)}), f32[128,32,64]{2,1,0:T(8,128)}) %all-gather.12.cloned.1.call-update) | async-done | bytes 1048592 | tf_op jit(solution)/shard_map/all_gather | solution.py:53
  204.6 30.1 %all-gather.14.cloned.1.call-done = f32[128,32,64]{2,0,1:T(8,128)} async-done(((f32[16,32,64]{2,0,1:T(8,128)}), f32[128,32,64]{2,0,1:T(8,128)}) %all-gather.14.cloned.1.call-update) | async-done | bytes 1048592 | tf_op jit(solution)/shard_map/all_gather | solution.py:56
  254.4 7.5 all-to-all-start.3
  262.7 25.2 %all-to-all-done.3 = f32[32,2,16,512]{3,1,2,0:T(2,128)} async-done(((f32[32,2,16,512]{3,1,2,0:T(2,128)}), f32[32,2,16,512]{3,1,2,0:T(2,128)}, u32[]{:S(2)}, u32[]{:S(2)}) %all-to-all-start.3) | async-done | bytes 2097184 | tf_op jit(solution)/shard_map/all_to_all | solution.py:67
  299.9 38.6 %all-gather.16.cloned.1.call-done = f32[128,32,64]{2,1,0:T(8,128)} async-done(((f32[16,32,64]{2,1,0:T(8,128)}), f32[128,32,64]{2,1,0:T(8,128)}) %all-gather.16.cloned.1.call-update) | async-done | bytes 1048592 | tf_op jit(solution)/shard_map/all_gather | solution.py:53
  344.5 7.7 all-to-all-start.4
  353.7 29.8 %all-gather.18.cloned.1.call-done = f32[128,32,64]{2,0,1:T(8,128)} async-done(((f32[16,32,64]{2,0,1:T(8,128)}), f32[128,32,64]{2,0,1:T(8,128)}) %all-gather.18.cloned.1.call-update) | async-done | bytes 1048592 | tf_op jit(solution)/shard_map/all_gather | solution.py:56
  403.1 7.5 all-to-all-start.5
  411.4 25.2 %all-to-all-done.5 = f32[32,2,16,512]{3,1,2,0:T(2,128)} async-done(((f32[32,2,16,512]{3,1,2,0:T(2,128)}), f32[32,2,16,512]{3,1,2,0:T(2,128)}, u32[]{:S(2)}, u32[]{:S(2)}) %all-to-all-start.5) | async-done | bytes 2097184 | tf_op jit(solution)/shard_map/all_to_all | solution.py:67
  449.9 8.0 fusion.34
  457.9 30.2 %all-gather.20.cloned.1.call-done = f32[128,32,64]{2,1,0:T(8,128)} async-done(((f32[16,32,64]{2,1,0:T(8,128)}), f32[128,32,64]{2,1,0:T(8,128)}) %all-gather.20.cloned.1.call-update) | async-done | bytes 1048592 | tf_op jit(solution)/shard_map/all_gather | solution.py:53
  492.6 38.5 %reduce-scatter.9.cloned.1.call-done = f32[16,32,64]{2,0,1:T(8,128)} async-done(((f32[128,32,64]{2,0,1:T(8,128)}), f32[16,32,64]{2,0,1:T(8,128)}) %reduce-scatter.9.cloned.1.call-update) | async-done | bytes 131088 | tf_op jit(solution)/shard_map/reduce_scatter | solution.py:107
  541.4 39.0 %reduce-scatter.11.cloned.1.call-done = f32[16,32,64]{2,1,0:T(8,128)} async-done(((f32[128,32,64]{2,1,0:T(8,128)}), f32[16,32,64]{2,1,0:T(8,128)}) %reduce-scatter.11.cloned.1.call-update) | async-done | bytes 131088 | tf_op jit(solution)/shard_map/reduce_scatter | solution.py:114
  590.0 32.7 %all_to_all.57 = f32[32,2,16,512]{3,1,2,0:T(2,128)S(1)} all-to-all(f32[32,2,16,512]{3,1,2,0:T(2,128)S(1)} %copy.93), channel_id=1, replica_groups=mesh['row'=8,'col'=32] {'col'}, dimensions={0} | all-to-all | bytes 4194304 | tf_op jit(solution)/shard_map/all_to_all | solution.py:93
  633.2 7.9 fusion.37
  641.4 39.7 %reduce-scatter.13.cloned.1.call-done = f32[16,32,64]{2,0,1:T(8,128)} async-done(((f32[128,32,64]{2,0,1:T(8,128)}), f32[16,32,64]{2,0,1:T(8,128)}) %reduce-scatter.13.cloned.1.call-update) | async-done | bytes 131088 | tf_op jit(solution)/shard_map/reduce_scatter | solution.py:107
  689.0 40.9 %reduce-scatter.15.cloned.1.call-done = f32[16,32,64]{2,1,0:T(8,128)} async-done(((f32[128,32,64]{2,1,0:T(8,128)}), f32[16,32,64]{2,1,0:T(8,128)}) %reduce-scatter.15.cloned.1.call-update) | async-done | bytes 131088 | tf_op jit(solution)/shard_map/reduce_scatter | solution.py:114
  739.5 32.9 %all_to_all.58 = f32[32,2,16,512]{3,1,2,0:T(2,128)S(1)} all-to-all(f32[32,2,16,512]{3,1,2,0:T(2,128)S(1)} %copy.99), channel_id=1, replica_groups=mesh['row'=8,'col'=32] {'col'}, dimensions={0} | all-to-all | bytes 4194304 | tf_op jit(solution)/shard_map/all_to_all | solution.py:93
  782.7 7.9 fusion.42
  790.7 40.1 %reduce-scatter.17.cloned.1.call-done = f32[16,32,64]{2,0,1:T(8,128)} async-done(((f32[128,32,64]{2,0,1:T(8,128)}), f32[16,32,64]{2,0,1:T(8,128)}) %reduce-scatter.17.cloned.1.call-update) | async-done | bytes 131088 | tf_op jit(solution)/shard_map/reduce_scatter | solution.py:107
  838.9 40.9 %reduce-scatter.19.cloned.1.call-done = f32[16,32,64]{2,1,0:T(8,128)} async-done(((f32[128,32,64]{2,1,0:T(8,128)}), f32[16,32,64]{2,1,0:T(8,128)}) %reduce-scatter.19.cloned.1.call-update) | async-done | bytes 131088 | tf_op jit(solution)/shard_map/reduce_scatter | solution.py:114
  889.4 32.8 %all_to_all.59 = f32[32,2,16,512]{3,1,2,0:T(2,128)S(1)} all-to-all(f32[32,2,16,512]{3,1,2,0:T(2,128)S(1)} %copy.105), channel_id=1, replica_groups=mesh['row'=8,'col'=32] {'col'}, dimensions={0} | all-to-all | bytes 4194304 | tf_op jit(solution)/shard_map/all_to_all | solution.py:93
  932.5 7.9 fusion.47
  941.4 39.1 %reduce-scatter.21.cloned.1.call-done = f32[16,32,64]{2,0,1:T(8,128)} async-done(((f32[128,32,64]{2,0,1:T(8,128)}), f32[16,32,64]{2,0,1:T(8,128)}) %reduce-scatter.21.cloned.1.call-update) | async-done | bytes 131088 | tf_op jit(solution)/shard_map/reduce_scatter | solution.py:107
  989.7 32.4 %all-gather.22.cloned.1.call-done = f32[128,32,64]{2,0,1:T(8,128)} async-done(((f32[16,32,64]{2,0,1:T(8,128)}), f32[128,32,64]{2,0,1:T(8,128)}) %all-gather.22.cloned.1.call-update) | async-done | bytes 1048592 | tf_op jit(solution)/shard_map/all_gather | solution.py:56
  1030.3 34.9 %reduce-scatter.23.cloned.1.call-done = f32[16,32,64]{2,1,0:T(8,128)} async-done(((f32[128,32,64]{2,1,0:T(8,128)}), f32[16,32,64]{2,1,0:T(8,128)}) %reduce-scatter.23.cloned.1.call-update) | async-done | bytes 131088 | tf_op jit(solution)/shard_map/reduce_scatter | solution.py:114
  (171 shorter events, 229.0 us)
Async XLA Ops:
  7.2 47.3 %all-gather.24.cloned.1.call-start = ((), (), s32[]{:S(2)}) async-start(), calls=%async_computation.32 | async-start | bytes 2359296 | tf_op jit(solution)/shard_map/all_gather | solution.py:53
  8.9 91.4 %all-gather.10.cloned.1.call-start = ((), (), s32[]{:S(2)}) async-start(), calls=%async_computation.17 | async-start | bytes 2359296 | tf_op jit(solution)/shard_map/all_gather | solution.py:56
  10.0 50.9 %copy-start.12 = (s32[3,32]{1,0:T(4,128)S(1)}, s32[3,32]{1,0:T(4,128)}, u32[]{:S(2)}) copy-start(s32[3,32]{1,0:T(4,128)} %param.12) | copy-start | bytes 1156
  10.0 50.9 %copy-start.11 = (s32[3,32,1]{1,2,0:T(1,128)S(1)}, s32[3,32,1]{1,2,0:T(1,128)}, u32[]{:S(2)}) copy-start(s32[3,32,1]{1,2,0:T(1,128)} %param.11) | copy-start | bytes 1156
  10.1 59.1 %copy-start.10 = (s32[4,7,32]{2,0,1:T(4,128)S(1)}, s32[4,7,32]{2,0,1:T(4,128)}, u32[]{:S(2)}) copy-start(s32[4,7,32]{2,0,1:T(4,128)} %param.10) | copy-start | bytes 10756
  61.8 50.4 %all-to-all-start = ((s32[32,1,2]{2,1,0:T(1,128)}), s32[32,1,2]{2,1,0:T(1,128)S(1)}, u32[]{:S(2)}, u32[]{:S(2)}) async-start(s32[32,1,2]{2,1,0:T(1,128)} %bitcast.5), calls=%async_computation | async-start | bytes 32768 | tf_op jit(solution)/shard_map/all_to_all | solution.py:68
  112.2 33.5 %all-to-all-start.1 = ((f32[32,2,16,512]{3,2,1,0:T(8,128)}), f32[32,2,16,512]{3,2,1,0:T(8,128)}, u32[]{:S(2)}, u32[]{:S(2)}) async-start(f32[32,2,16,512]{3,2,1,0:T(8,128)} %copy.69), calls=%async_computation.1 | async-start | bytes 4194304 | tf_op jit(solution)/shard_map/all_to_all | solution.py:67
  119.7 69.9 %all-gather.12.cloned.1.call-start = ((), (), s32[]{:S(2)}) async-start(), calls=%async_computation.18 | async-start | bytes 2359296 | tf_op jit(solution)/shard_map/all_gather | solution.py:53
  151.0 83.7 %all-gather.14.cloned.1.call-start = ((), (), s32[]{:S(2)}) async-start(), calls=%async_computation.19 | async-start | bytes 2359296 | tf_op jit(solution)/shard_map/all_gather | solution.py:56
  195.7 58.7 %all-to-all-start.2 = ((s32[32,1,2]{2,1,0:T(1,128)}), s32[32,1,2]{2,1,0:T(1,128)S(1)}, u32[]{:S(2)}, u32[]{:S(2)}) async-start(s32[32,1,2]{2,1,0:T(1,128)} %bitcast.22), calls=%async_computation.2 | async-start | bytes 32768 | tf_op jit(solution)/shard_map/all_to_all | solution.py:68
  254.4 33.5 %all-to-all-start.3 = ((f32[32,2,16,512]{3,1,2,0:T(2,128)}), f32[32,2,16,512]{3,1,2,0:T(2,128)}, u32[]{:S(2)}, u32[]{:S(2)}) async-start(f32[32,2,16,512]{3,1,2,0:T(2,128)} %copy.77), calls=%async_computation.3 | async-start | bytes 4194304 | tf_op jit(solution)/shard_map/all_to_all | solution.py:67
  261.9 76.6 %all-gather.16.cloned.1.call-start = ((), (), s32[]{:S(2)}) async-start(), calls=%async_computation.20 | async-start | bytes 2359296 | tf_op jit(solution)/shard_map/all_gather | solution.py:53
  299.8 83.7 %all-gather.18.cloned.1.call-start = ((), (), s32[]{:S(2)}) async-start(), calls=%async_computation.21 | async-start | bytes 2359296 | tf_op jit(solution)/shard_map/all_gather | solution.py:56
  344.5 58.6 %all-to-all-start.4 = ((s32[32,1,2]{2,1,0:T(1,128)}), s32[32,1,2]{2,1,0:T(1,128)S(1)}, u32[]{:S(2)}, u32[]{:S(2)}) async-start(s32[32,1,2]{2,1,0:T(1,128)} %bitcast.37), calls=%async_computation.4 | async-start | bytes 32768 | tf_op jit(solution)/shard_map/all_to_all | solution.py:68
  403.1 33.5 %all-to-all-start.5 = ((f32[32,2,16,512]{3,1,2,0:T(2,128)}), f32[32,2,16,512]{3,1,2,0:T(2,128)}, u32[]{:S(2)}, u32[]{:S(2)}) async-start(f32[32,2,16,512]{3,1,2,0:T(2,128)} %copy.85), calls=%async_computation.5 | async-start | bytes 4194304 | tf_op jit(solution)/shard_map/all_to_all | solution.py:67
  410.6 77.5 %all-gather.20.cloned.1.call-start = ((), (), s32[]{:S(2)}) async-start(), calls=%async_computation.22 | async-start | bytes 2359296 | tf_op jit(solution)/shard_map/all_gather | solution.py:53
  449.5 81.6 %reduce-scatter.9.cloned.1.call-start = ((), (), s32[]{:S(2)}) async-start(), calls=%async_computation.23 | async-start | bytes 2359296 | tf_op jit(solution)/shard_map/reduce_scatter | solution.py:107
  457.9 122.5 %reduce-scatter.11.cloned.1.call-start = ((), (), s32[]{:S(2)}) async-start(), calls=%async_computation.24 | async-start | bytes 2359296 | tf_op jit(solution)/shard_map/reduce_scatter | solution.py:114
  492.6 46.3 %copy-start.4 = (f32[16,32,64]{2,0,1:T(8,128)}, f32[16,32,64]{2,0,1:T(8,128)S(1)}, u32[]{:S(2)}) copy-start(f32[16,32,64]{2,0,1:T(8,128)S(1)} %fusion.65) | copy-start | bytes 393220
  538.9 142.1 %reduce-scatter.13.cloned.1.call-start = ((), (), s32[]{:S(2)}) async-start(), calls=%async_computation.25 | async-start | bytes 2359296 | tf_op jit(solution)/shard_map/reduce_scatter | solution.py:107
  641.1 40.0 %copy-start.5 = (f32[16,32,64]{2,0,1:T(8,128)S(1)}, f32[16,32,64]{2,0,1:T(8,128)}, u32[]{:S(2)}) copy-start(f32[16,32,64]{2,0,1:T(8,128)} %fusion.62) | copy-start | bytes 393220
  641.2 88.8 %reduce-scatter.15.cloned.1.call-start = ((), (), s32[]{:S(2)}) async-start(), calls=%async_computation.26 | async-start | bytes 2359296 | tf_op jit(solution)/shard_map/reduce_scatter | solution.py:114
  689.0 141.8 %reduce-scatter.17.cloned.1.call-start = ((), (), s32[]{:S(2)}) async-start(), calls=%async_computation.27 | async-start | bytes 2359296 | tf_op jit(solution)/shard_map/reduce_scatter | solution.py:107
  790.6 40.1 %copy-start.3 = (f32[16,32,64]{2,0,1:T(8,128)S(1)}, f32[16,32,64]{2,0,1:T(8,128)}, u32[]{:S(2)}) copy-start(f32[16,32,64]{2,0,1:T(8,128)} %fusion.59) | copy-start | bytes 393220
  790.6 89.1 %reduce-scatter.19.cloned.1.call-start = ((), (), s32[]{:S(2)}) async-start(), calls=%async_computation.28 | async-start | bytes 2359296 | tf_op jit(solution)/shard_map/reduce_scatter | solution.py:114
  838.6 141.8 %reduce-scatter.21.cloned.1.call-start = ((), (), s32[]{:S(2)}) async-start(), calls=%async_computation.29 | async-start | bytes 2359296 | tf_op jit(solution)/shard_map/reduce_scatter | solution.py:107
  940.4 40.0 %copy-start.6 = (f32[16,32,64]{2,0,1:T(8,128)S(1)}, f32[16,32,64]{2,0,1:T(8,128)}, u32[]{:S(2)}) copy-start(f32[16,32,64]{2,0,1:T(8,128)} %convolution_bitcast_fusion.9) | copy-start | bytes 393220
  940.5 81.7 %all-gather.22.cloned.1.call-start = ((), (), s32[]{:S(2)}) async-start(), calls=%async_computation.31 | async-start | bytes 2359296 | tf_op jit(solution)/shard_map/all_gather | solution.py:56
  941.1 124.1 %reduce-scatter.23.cloned.1.call-start = ((), (), s32[]{:S(2)}) async-start(), calls=%async_computation.30 | async-start | bytes 2359296 | tf_op jit(solution)/shard_map/reduce_scatter | solution.py:114
  1028.5 36.6 %copy-start.7 = (f32[16,32,64]{2,1,0:T(8,128)S(1)}, f32[16,32,64]{2,1,0:T(8,128)}, u32[]{:S(2)}) copy-start(f32[16,32,64]{2,1,0:T(8,128)} %reduce-scatter.11.cloned.1.call-done) | copy-start | bytes 393220
  1028.5 36.6 %copy-start.8 = (f32[16,32,64]{2,1,0:T(8,128)S(1)}, f32[16,32,64]{2,1,0:T(8,128)}, u32[]{:S(2)}) copy-start(f32[16,32,64]{2,1,0:T(8,128)} %reduce-scatter.15.cloned.1.call-done) | copy-start | bytes 393220
  1028.5 36.6 %copy-start.9 = (f32[16,32,64]{2,1,0:T(8,128)S(1)}, f32[16,32,64]{2,1,0:T(8,128)}, u32[]{:S(2)}) copy-start(f32[16,32,64]{2,1,0:T(8,128)} %reduce-scatter.19.cloned.1.call-done) | copy-start | bytes 393220
  (3 other events, 35.3 us)
Sparse Core Ops, SparseCore 0:
  10.4 44.0 all-gather.23
  60.7 39.6 all-gather.9
  151.1 38.4 all-gather.11
  195.0 39.6 all-gather.13
  299.9 38.4 all-gather.15
  343.8 39.6 all-gather.17
  449.6 38.4 all-gather.19
  490.6 40.4 reduce-scatter.8
  539.1 41.2 reduce-scatter.10
  641.3 39.7 reduce-scatter.12
  689.1 40.8 reduce-scatter.14
  790.8 39.9 reduce-scatter.16
  838.8 40.9 reduce-scatter.18
  940.6 39.8 reduce-scatter.20
  982.1 40.0 all-gather.21
  1024.6 40.4 reduce-scatter.22
where the time goes:
time: 1080 us; the launch traced here: 1070 us
  waiting for transfers between devices  654 us (61%)
  local copies, waits for them, and re-layouts  131 us (12%)
  matrix products  117 us (11%)
  blocking collectives  98.4 us (9%)
  starting transfers between devices  47.2 us (4%)
  between operations  14.8 us (1%)
  other arithmetic  11.6 us (1%)
    reduce_scatter x4, waiting for transfers between devices, per_device(): lax.psum_scatter(jnp.einsum('dkib,ikdr->bkr', piece, masked, precision=hi...  157 us
    reduce_scatter x4, waiting for transfers between devices, per_device(): lax.psum_scatter(jnp.einsum('kic,ikr->ckr', diagonal_piece, reduced, prec...  156 us
    all_gather x4, waiting for transfers between devices, per_device(): gathered = lax.all_gather(residual, 'row', axis=0, tiled=True)  152 us
    all_gather x4, waiting for transfers between devices, per_device(): solved_all = lax.all_gather(solved_rows, 'row', axis=0, tiled=True)  114 us
    all_to_all x3, blocking collectives, per_device(): lax.all_to_all(spread(receiver, downward).reshape(col_count, capacity, ro...  98.4 us
    all_to_all x3, waiting for transfers between devices, per_device(): lax.all_to_all(packed, 'col', split_axis=0, concat_axis=0, tiled=True)  74.8 us
    dot_general x4, matrix products, per_device(): jnp.einsum('dkib,ikdr->bkr', piece, masked, precision=highest)  31.7 us
    all_to_all x3, starting transfers between devices, per_device(): lax.all_to_all(parent_ids.reshape(col_count, capacity), 'col', split_axis...  22.5 us
  transfers between devices with their start and end apart: 22, of which 19 were waited for; matrix products, arithmetic and copies ran while one was open for 9% of the time, Pallas kernels for 0%

commit v1 on v0

v1 whole, which is shorter than its diff:
```python
import functools

import jax
import jax.numpy as jnp
from jax import lax
from jax.experimental import pallas as pl
from jax.experimental.pallas import tpu as pltpu
from jax.sharding import PartitionSpec as P

F32 = jnp.float32
BF16 = jnp.bfloat16
LEVELS = 4
ANC = 8
SUP = 32
SLOTS = 64
NR = 8
OWN = SUP // NR
FWD_GROUPS = ((0, 1), (1, 2), (2, 8))
BWD_GROUPS = (((0, 1), (1, 2), (2, 3), (3, 8)), ((0, 1), (1, 2), (2, 8)), ((0, 1), (1, 8)))
FSRC, POS, PREV, LAST, BSRC = range(5)


def low_lanes(shape):
    return lax.broadcasted_iota(jnp.int32, shape, len(shape) - 1) < 64


def swap_halves(x):
    return pltpu.roll(x.reshape(-1, 128), 64, 1).reshape(x.shape)


def split(x):
    high = x.astype(BF16).astype(F32)
    return high, x - high


def store_matrix(block):
    wide = jnp.concatenate([block[:8], block[8:]], axis=1)
    high, low = split(wide)
    return jnp.concatenate([high, low], axis=0).astype(BF16)


def expand(packed):
    low = low_lanes((8, 128))
    rolled = swap_halves(packed)
    zero = jnp.zeros((8, 128), F32)
    top, bottom = [], []
    for z in range(8):
        top += [jnp.where(low, packed[z], zero), jnp.where(low, rolled[z], zero)]
        bottom += [jnp.where(low, zero, rolled[z]), jnp.where(low, zero, packed[z])]
    high, rest = split(jnp.concatenate(top + bottom, axis=0))
    return jnp.concatenate([high.astype(BF16), rest.astype(BF16)], axis=1)


def apply(matrix, weights):
    o = jnp.dot(matrix, weights, preferred_element_type=F32).reshape(8, 2, 8, 256)
    return o[:, 0, :, :128] + o[:, 0, :, 128:] + o[:, 1, :, :128]


def apply_t(matrix, tiles):
    count = tiles.shape[0]
    high, rest = split(tiles)
    zero = jnp.zeros((8, 128), F32)
    rows = []
    for d in range(count):
        rows.append(jnp.concatenate([high[d], rest[d]], axis=1))
        rows.append(jnp.concatenate([high[d], zero], axis=1))
    weights = jnp.concatenate(rows, axis=0).astype(BF16)
    o = lax.dot_general(matrix, weights, (((0,), (0,)), ((), ())), preferred_element_type=F32)
    c = (o[:, :128] + o[:, 128:]).reshape(2, 8, 2, 8, 128)
    low = low_lanes((8, 8, 128))
    direct = jnp.where(low, c[0, :, 0], c[1, :, 1])
    cross = jnp.where(low, c[0, :, 1], c[1, :, 0])
    return direct + swap_halves(cross)


def kernel(
    ncol, tab, pat, rhs, anc, dinv, panels, sol_out, bu_out,
    stage, ph, dv, dh, rsend, rs, sol, out, car, cum, fsend, frecv, bsend, brecv, anct,
    part, rsr, tot, xsend, solr,
    sem_stage, sem_dv, sem_r, sem_ag_s, sem_ag_r, sem_fs, sem_fr, sem_bs, sem_br, sem_rs_s, sem_rs_r, sem_x,
):
    row, col = lax.axis_index("row"), lax.axis_index("col")
    cap = SLOTS // ncol
    right, left = lax.rem(row + 1, NR), lax.rem(row + NR - 1, NR)

    def rowdev(z):
        return {"row": z}

    def at_row(offset):
        return lax.rem(row + offset + 2 * NR, NR)

    barrier = pltpu.get_barrier_semaphore()

    @pl.loop(1, NR)
    def _(k):
        pl.semaphore_signal(barrier, inc=1, device_id=rowdev(lax.rem(row + k, NR)), device_id_type=pl.DeviceIdType.MESH)

    @pl.loop(1, ncol)
    def _(k):
        pl.semaphore_signal(barrier, inc=1, device_id={"col": lax.rem(col + k, ncol)}, device_id_type=pl.DeviceIdType.MESH)

    def load_panels(l):
        return pltpu.make_async_copy(panels.at[l], stage.at[l % 2], sem_stage.at[l % 2])

    load_panels(0).start()
    load_panels(1).start()
    pl.semaphore_wait(barrier, NR - 1 + ncol - 1)

    def row_send(src, dst, send_sem, recv_sem):
        @pl.loop(1, NR)
        def _(k):
            z = lax.rem(row + k, NR)
            pltpu.make_async_remote_copy(
                src_ref=src(z), dst_ref=dst(row), send_sem=send_sem, recv_sem=recv_sem,
                device_id=rowdev(z), device_id_type=pl.DeviceIdType.MESH,
            ).start()

    def wait_bytes(ref, sem):
        pltpu.make_async_copy(ref, ref, sem).wait()

    def dinv_send(l):
        row_send(lambda z: dinv.at[l, pl.ds(z * OWN, OWN)], lambda o: dv.at[l, o], sem_dv.at[0, l], sem_dv.at[1, l])
        pltpu.make_async_copy(dinv.at[l, pl.ds(row * OWN, OWN)], dv.at[l, row], sem_dv.at[2, l]).start()

    def dinv_wait(l):
        wait_bytes(dv.at[l, pl.ds(0, NR - 1)], sem_dv.at[0, l])
        wait_bytes(dv.at[l, pl.ds(0, NR - 1)], sem_dv.at[1, l])
        wait_bytes(dv.at[l, 0], sem_dv.at[2, l])
        for j in range(OWN):
            for z in range(NR):
                dh[l, j, 16 * z : 16 * z + 16, :] = store_matrix(dv[l, z, j])

    def r_send(l):
        rs[l, row] = rsend[l, row]
        row_send(lambda z: rsend.at[l, z], lambda o: rs.at[l, o], sem_r.at[0, l], sem_r.at[1, l])

    def r_wait(l):
        wait_bytes(rs.at[l, pl.ds(0, NR - 1)], sem_r.at[0, l])
        wait_bytes(rs.at[l, pl.ds(0, NR - 1)], sem_r.at[1, l])

    def col_send(src, dst, send_sem, recv_sem):
        @pl.loop(1, ncol)
        def _(k):
            c = lax.rem(col + k, ncol)
            pltpu.make_async_remote_copy(
                src_ref=src.at[pl.ds(c * cap, cap)], dst_ref=dst.at[pl.ds(col * cap, cap)],
                send_sem=send_sem, recv_sem=recv_sem,
                device_id={"col": c}, device_id_type=pl.DeviceIdType.MESH,
            ).start()
        dst[pl.ds(col * cap, cap)] = src[pl.ds(col * cap, cap)]

    def col_wait(dst, sem):
        wait_bytes(dst.at[pl.ds(0, SLOTS - cap)], sem)

    def fwd_pack_send(l, g):
        a, b = FWD_GROUPS[g]
        src, dst = fsend[g], frecv[g].at[l]

        @pl.loop(0, SLOTS, unroll=4)
        def _(s):
            k = tab[l, FSRC, s]
            if l == 0 or a == 7:
                src[s] = out[k, pl.ds(a, b - a)]
            else:
                src[s] = out[k, pl.ds(a, b - a)] + car[k, pl.ds(a, b - a)]
        col_send(src, dst, sem_fs.at[l, g], sem_fr.at[l, g])

    def fwd_collect(l, g):
        a, b = FWD_GROUPS[g]
        dst = frecv[g].at[l]
        col_wait(dst, sem_fr.at[l, g])
        col_wait(fsend[g], sem_fs.at[l, g])

        @pl.loop(0, SLOTS, unroll=4)
        def _(s):
            cum[s, pl.ds(0, b - a)] = dst[s] + cum[tab[l, PREV, s], pl.ds(0, b - a)]

        if g == 0:
            @pl.loop(0, SUP, unroll=4)
            def _(p):
                rsend[l + 1, p // OWN, p % OWN] = rhs[l + 1, p] - cum[tab[l, LAST, p], 0]
        else:
            @pl.loop(0, SUP, unroll=4)
            def _(p):
                car[p, pl.ds(a - 1, b - a)] = cum[tab[l, LAST, p], pl.ds(0, b - a)]

    def bwd_pack_send(l, g, source):
        src, dst = bsend[l][g], brecv[l][g]

        @pl.loop(0, SLOTS, unroll=4)
        def _(s):
            src[s] = source(tab[l, BSRC, s])
        col_send(src, dst, sem_bs.at[l, g], sem_br.at[l, g])

    def bwd_gather(l, g):
        a, b = BWD_GROUPS[l][g]
        dst = brecv[l][g]
        col_wait(dst, sem_br.at[l, g])
        col_wait(bsend[l][g], sem_bs.at[l, g])

        @pl.loop(0, SUP, unroll=4)
        def _(k):
            anct[l, k, pl.ds(a, b - a)] = dst[tab[l, POS, k]]

    def convert(l):
        load_panels(l).wait()

        @pl.loop(0, SUP)
        def _(g):
            for d in range(ANC):
                block = stage[l % 2, d, g]
                if d > 0:
                    block = block * pat[l, d - 1, g].astype(F32)
                ph[l, g, 16 * d : 16 * d + 16, :] = store_matrix(block)
        if l + 2 < LEVELS:
            load_panels(l + 2).start()

    def ag_copy(l, c, t, way):
        origin = at_row(1 - t) if way == 0 else at_row(t - 1)
        return pltpu.make_async_remote_copy(
            src_ref=sol.at[l, origin, c], dst_ref=sol.at[l, origin, c],
            send_sem=sem_ag_s.at[l, c, t - 1, way], recv_sem=sem_ag_r.at[l, c, t - 1, way],
            device_id=rowdev(right if way == 0 else left), device_id_type=pl.DeviceIdType.MESH,
        )

    def ag_ways(c, t):
        return (0, 1) if t < 4 else (c % 2,)

    def product(l, g):
        out[g] = apply(ph[l, g], expand(sol[l, g // OWN, g % OWN].reshape(8, 8, 128)))

    def solve(l):
        r_wait(l)
        for c in range(OWN):
            sol[l, row, c] = apply(dh[l, c], expand(rs[l, :, c])).reshape(64, 128)
            for way in ag_ways(c, 1):
                ag_copy(l, c, 1, way).start()

    def spread_solved(l):
        @pl.loop(0, OWN)
        def _(c):
            product(l, row * OWN + c)
        for t in range(1, 5):
            for c in range(OWN):
                for way in ag_ways(c, t):
                    ag_copy(l, c, t, way).wait_recv()
                    if t < 4 and way in ag_ways(c, t + 1):
                        ag_copy(l, c, t + 1, way).start()
                if t == 4:
                    product(l, at_row(4) * OWN + c)
                else:
                    @pl.loop(0, 2)
                    def _(w):
                        product(l, lax.rem(row + NR - t + 2 * t * w, NR) * OWN + c)
        for t in range(1, 5):
            for c in range(OWN):
                for way in ag_ways(c, t):
                    ag_copy(l, c, t, way).wait_send()

    def rs_dest(t, way):
        return at_row(5 - t) if way == 0 else at_row(t - 5)

    def rs_ways(c, t):
        return (0, 1) if t > 1 else (c % 2,)

    def rs_copy(l, c, t, way):
        first = t == 1 or way not in rs_ways(c, t - 1)
        src = part.at[rs_dest(t, way), c] if first else rsr.at[l, way, t - 2, c]
        return pltpu.make_async_remote_copy(
            src_ref=src, dst_ref=rsr.at[l, way, t - 1, c],
            send_sem=sem_rs_s.at[l, c, t - 1, way], recv_sem=sem_rs_r.at[l, c, t - 1, way],
            device_id=rowdev(right if way == 0 else left), device_id_type=pl.DeviceIdType.MESH,
        )

    def sum_over_row(l, make):
        for t in range(1, 5):
            if t == 1:
                for c in range(OWN):
                    make(at_row(4) * OWN + c)
            else:
                for c in range(OWN):
                    @pl.loop(0, 2)
                    def _(w):
                        make(lax.rem(row + NR + (5 - t) * (1 - 2 * w), NR) * OWN + c)
            for c in range(OWN):
                for way in rs_ways(c, t):
                    if t > 1 and way in rs_ways(c, t - 1):
                        rs_copy(l, c, t - 1, way).wait_recv()
                        rsr[l, way, t - 2, c] += part[rs_dest(t, way), c]
                    rs_copy(l, c, t, way).start()
        for c in range(OWN):
            make(row * OWN + c)
        for c in range(OWN):
            for way in (0, 1):
                rs_copy(l, c, 4, way).wait_recv()
            tot[l, c] = part[row, c] + rsr[l, 0, 3, c] + rsr[l, 1, 3, c]
        for c in range(OWN):
            for t in range(1, 5):
                for way in rs_ways(c, t):
                    rs_copy(l, c, t, way).wait_send()

    def finish(l):
        for c in range(OWN):
            reduced = (sol[l, row, c] - tot[l, c]).reshape(8, 8, 128)
            xsend[l, :, c] = apply_t(dh[l, c], reduced)
        solr[l, row] = xsend[l, row]
        row_send(lambda z: xsend.at[l, z], lambda o: solr.at[l, o], sem_x.at[0, l], sem_x.at[1, l])
        wait_bytes(solr.at[l, pl.ds(0, NR - 1)], sem_x.at[1, l])
        wait_bytes(solr.at[l, pl.ds(0, NR - 1)], sem_x.at[0, l])

    def emit(l):
        sol_out[l] = solr[l].reshape(SUP, 8, 128)

    def set_part(g, value):
        part[g // OWN, g % OWN] = value.reshape(64, 128)

    for l in range(LEVELS):
        dinv_send(l)
    rsend[0] = rhs[0].reshape(NR, OWN, 8, 128)
    r_send(0)
    cum[SLOTS] = jnp.zeros(cum.shape[1:], F32)
    bwd_pack_send(2, 1, lambda k: anc[k, pl.ds(0, 7)])
    convert(0)
    dinv_wait(0)
    for l in range(LEVELS - 1):
        solve(l)
        spread_solved(l)
        if l > 0:
            fwd_collect(l - 1, 1)
        fwd_pack_send(l, 0)
        if l > 0:
            fwd_collect(l - 1, 2)

            @pl.loop(0, SUP)
            def _(g):
                car[g, 7] = jnp.zeros((8, 128), F32)
        fwd_pack_send(l, 1)
        fwd_pack_send(l, 2)
        convert(l + 1)
        dinv_wait(l + 1)
        if l == 0:
            bwd_gather(2, 1)
            bwd_pack_send(1, 2, lambda k: anct[2, k, pl.ds(1, 6)])
        if l == 1:
            bwd_gather(1, 2)
            bwd_pack_send(0, 3, lambda k: anct[1, k, pl.ds(2, 5)])
        if l == 2:
            sum_over_row(3, lambda g: set_part(g, apply_t(ph[3, g], anc[g])))
        fwd_collect(l, 0)
        r_send(l + 1)

    solve(3)
    finish(3)
    bwd_pack_send(2, 0, lambda k: solr[3, k // OWN, pl.ds(k % OWN, 1)])
    emit(3)
    spread_solved(3)
    fwd_collect(2, 1)
    fwd_collect(2, 2)

    @pl.loop(0, SUP)
    def _(g):
        bu_out[g, pl.ds(0, 7)] = out[g, pl.ds(0, 7)] + car[g, pl.ds(0, 7)]
        bu_out[g, 7] = out[g, 7]

    for l in (2, 1, 0):
        if l == 1:
            bwd_gather(1, 1)
        if l == 0:
            bwd_gather(0, 3)
            bwd_gather(0, 2)
            bwd_gather(0, 1)

        @pl.loop(0, SUP)
        def _(g):
            set_part(g, apply_t(ph[l, g, 16:, :], anct[l, g, pl.ds(1, 7)]))
        bwd_gather(l, 0)
        if l == 2:
            bwd_pack_send(1, 1, lambda k: anct[2, k, pl.ds(0, 1)])
        if l == 1:
            bwd_pack_send(0, 1, lambda k: anct[1, k, pl.ds(0, 1)])
            bwd_pack_send(0, 2, lambda k: anct[1, k, pl.ds(1, 1)])

        def add_part(g):
            extra = apply_t(ph[l, g, 0:16, :], anct[l, g, pl.ds(0, 1)])
            part[g // OWN, g % OWN] += extra.reshape(64, 128)
        sum_over_row(l, add_part)
        finish(l)
        if l > 0:
            bwd_pack_send(l - 1, 0, lambda k: solr[l, k // OWN, pl.ds(k % OWN, 1)])
        emit(l)


def tables(parent_owner, parent_local, ncol):
    cap = SLOTS // ncol
    owner = parent_owner[:, :, 0]
    here = jnp.arange(SUP, dtype=jnp.int32)
    same = (owner[:, :, None] == owner[:, None, :]) & (here[None, :, None] < here[None, None, :])
    pos = owner * cap + jnp.sum(same.astype(jnp.int32), axis=1)
    slots = jnp.arange(SLOTS, dtype=jnp.int32)
    hit = pos[:, None, :] == slots[None, :, None]
    fsrc = jnp.sum(jnp.where(hit, here[None, None, :], 0), axis=2)
    ids = jnp.sum(jnp.where(hit, parent_local[:, None, :] + 1, 0), axis=2)
    ids = lax.all_to_all(ids.reshape(3, ncol, cap), "col", split_axis=1, concat_axis=1, tiled=True).reshape(3, SLOTS)
    equal = (ids[:, :, None] == ids[:, None, :]) & (slots[None, None, :] < slots[None, :, None])
    prev = jnp.max(jnp.where(equal, slots[None, None, :], -1), axis=2)
    prev = jnp.where(prev < 0, SLOTS, prev)
    mine = ids[:, None, :] == here[None, :, None] + 1
    last = jnp.max(jnp.where(mine, slots[None, None, :], -1), axis=2)
    last = jnp.where(last < 0, SLOTS, last)
    bsrc = jnp.maximum(ids - 1, 0)
    wide = lambda x: jnp.pad(x, ((0, 0), (0, SLOTS - x.shape[1])))
    return jnp.stack([fsrc, wide(pos), prev, wide(last), bsrc], axis=1)


def per_device(ncol, rhs, dinv, panels, pattern, parent_owner, parent_local, ancestor_solution):
    tab = tables(parent_owner, parent_local, ncol)
    rhs_p = rhs.reshape(LEVELS, 2, 8, SUP, 64).transpose(0, 3, 2, 1, 4).reshape(LEVELS, SUP, 8, 128)
    anc_p = ancestor_solution.reshape(2, 8, SUP, ANC, 64).transpose(2, 3, 1, 0, 4).reshape(SUP, ANC, 8, 128)
    vmem = pl.BlockSpec(memory_space=pltpu.VMEM)
    smem = pl.BlockSpec(memory_space=pltpu.SMEM)
    anywhere = pl.BlockSpec(memory_space=pl.ANY)
    sems = pltpu.SemaphoreType.DMA
    tile = (8, 128)
    fsend = tuple(pltpu.VMEM((SLOTS, b - a) + tile, F32) for a, b in FWD_GROUPS)
    frecv = tuple(pltpu.VMEM((3, SLOTS, b - a) + tile, F32) for a, b in FWD_GROUPS)
    bbuf = tuple(tuple(pltpu.VMEM((SLOTS, b - a) + tile, F32) for a, b in groups) for groups in BWD_GROUPS)
    sol, bu = pl.pallas_call(
        functools.partial(kernel, ncol),
        out_shape=(
            jax.ShapeDtypeStruct((LEVELS, SUP) + tile, F32),
            jax.ShapeDtypeStruct((SUP, ANC) + tile, F32),
        ),
        in_specs=[smem, smem, vmem, vmem, anywhere, anywhere],
        out_specs=(vmem, vmem),
        scratch_shapes=[
            pltpu.VMEM((2, ANC, SUP, 16, 128), F32),
            pltpu.VMEM((LEVELS, SUP, 128, 256), BF16),
            pltpu.VMEM((LEVELS, NR, OWN, 16, 128), F32),
            pltpu.VMEM((LEVELS, OWN, 128, 256), BF16),
            pltpu.VMEM((LEVELS, NR, OWN) + tile, F32),
            pltpu.VMEM((LEVELS, NR, OWN) + tile, F32),
            pltpu.VMEM((LEVELS, NR, OWN, 64, 128), F32),
            pltpu.VMEM((SUP, ANC) + tile, F32),
            pltpu.VMEM((SUP, ANC) + tile, F32),
            pltpu.VMEM((SLOTS + 1, 6) + tile, F32),
            fsend, frecv, bbuf, bbuf,
            pltpu.VMEM((3, SUP, ANC) + tile, F32),
            pltpu.VMEM((NR, OWN, 64, 128), F32),
            pltpu.VMEM((LEVELS, 2, 4, OWN, 64, 128), F32),
            pltpu.VMEM((LEVELS, OWN, 64, 128), F32),
            pltpu.VMEM((LEVELS, NR, OWN) + tile, F32),
            pltpu.VMEM((LEVELS, NR, OWN) + tile, F32),
            sems((2,)), sems((3, LEVELS)), sems((2, LEVELS)),
            sems((LEVELS, OWN, 4, 2)), sems((LEVELS, OWN, 4, 2)),
            sems((3, 3)), sems((3, 3)), sems((3, 4)), sems((3, 4)),
            sems((LEVELS, OWN, 4, 2)), sems((LEVELS, OWN, 4, 2)), sems((2, LEVELS)),
        ],
        compiler_params=pltpu.CompilerParams(
            collective_id=0, has_side_effects=True, vmem_limit_bytes=60 * 1024 * 1024
        ),
        cost_estimate=pl.CostEstimate(flops=4 * 10**9, bytes_accessed=12 * 10**6, transcendentals=0),
    )(tab, pattern, rhs_p, anc_p, dinv, panels)
    solution = sol.reshape(LEVELS, SUP, 8, 2, 64).transpose(0, 3, 2, 1, 4).reshape(LEVELS, 16, SUP, 64)
    boundary = bu.reshape(SUP, ANC, 8, 2, 64).transpose(3, 2, 0, 1, 4).reshape(16, SUP, ANC, 64)
    return solution, boundary


def solution(mesh):
    placed = (
        P(None, "row", "col", None),
        P(None, "col", "row", None),
        P(None, None, "col", "row", None),
        P(None, None, "col"),
        P(None, "col", None),
        P(None, "col"),
        P("row", "col", None, None),
    )
    return jax.shard_map(
        functools.partial(per_device, mesh.shape["col"]),
        mesh=mesh,
        in_specs=placed,
        out_specs=(P(None, "row", "col", None), P("row", "col", None, None)),
        check_vma=False,
    )
```

time: 1080 us -> 331 us (0.31)
  waiting for transfers between devices: 654 us -> 0.01 us
  Pallas kernels: 0 us -> 304 us
  matrix products: 117 us -> 0 us
  local copies, waits for them, and re-layouts: 131 us -> 17.1 us
  blocking collectives: 98.4 us -> 0 us
  starting transfers between devices: 47.2 us -> 7.62 us
  between operations: 14.8 us -> 0.77 us
    reduce_scatter x8 -> x0, waiting for transfers between devices: 313 us -> none  [the longest x4 157 us: per_device(): lax.psum_scatter(jnp.einsum('dkib,ikdr->bkr', piece, masked, precision=hi...]
    pallas_call x0 -> x1, Pallas kernels: none -> 304 us  [per_device(): pl.pallas_call(functools.partial(kernel, ncol), out_shape=(jax.ShapeDtype...]
    all_gather x8 -> x0, waiting for transfers between devices: 266 us -> none  [the longest x4 152 us: per_device(): gathered = lax.all_gather(residual, 'row', axis=0, tiled=True)]
    dot_general x28 -> x0, matrix products: 117 us -> none  [the longest x4 31.7 us: per_device(): jnp.einsum('dkib,ikdr->bkr', piece, masked, precision=highest)]
    all_to_all x3 -> x0, blocking collectives: 98.4 us -> none  [per_device(): lax.all_to_all(spread(receiver, downward).reshape(col_count, capacity, ro...]
    all_to_all x6 -> x1, waiting for transfers between devices: 74.8 us -> 0.01 us  [tables(): lax.all_to_all(ids.reshape(3, ncol, cap), 'col', split_axis=1, concat_axi...]
    reshape x24 -> x7, local copies, waits for them, and re-layouts: 67.6 us -> 11.6 us  [the longest x2 5.34 us: per_device(): ancestor_solution.reshape(2, 8, SUP, ANC, 64).transpose(2, 3, 1, 0, 4)]
    all_to_all x6 -> x1, starting transfers between devices: 45 us -> 7.62 us  [tables(): lax.all_to_all(ids.reshape(3, ncol, cap), 'col', split_axis=1, concat_axi...]
  transfers between devices with their start and end apart: 22 -> 1, of which waited for: 19 -> 0; matrix products, arithmetic and copies ran while one was open for 9% -> 2% of each run, Pallas kernels for 0% -> 0%
where the time goes in v1:
time: 331 us
  Pallas kernels  304 us (92%)
  local copies, waits for them, and re-layouts  17.1 us (5%)
  starting transfers between devices  7.62 us (2%)
    pallas_call x1, Pallas kernels, per_device(): pl.pallas_call(functools.partial(kernel, ncol), out_shape=(jax.ShapeDtype...  304 us
    all_to_all x1, starting transfers between devices, tables(): lax.all_to_all(ids.reshape(3, ncol, cap), 'col', split_axis=1, concat_axi...  7.62 us
  transfers between devices with their start and end apart: 1, of which 0 were waited for; matrix products, arithmetic and copies ran while one was open for 2% of the time, Pallas kernels for 0%

profile of v1, /device:TPU:2, one launch (start us, length us, event | category | flops | bytes accessed | tf_op | source)
XLA Modules:
  0.0 330.9 jit_solution(9934006890765815275)
XLA Ops:
  0.6 0.7 copy.58
  1.3 0.1 convert_reduce_fusion
  1.4 0.7 multiply_add_fusion
  2.1 0.1 select_reduce_fusion.2
  2.2 0.7 copy.48
  2.9 7.6 %all-to-all-start = ((s32[3,32,2]{0,2,1:T(2,128)}), s32[3,32,2]{0,2,1:T(2,128)S(1)}, u32[]{:S(2)}, u32[]{:S(2)}) async-start(s32[3,32,2]{0,2,1:T(2,128)} %bitcast), calls=%async_computation | async-start | bytes 65536 | tf_op jit(solution)/shard_map/all_to_all | solution.py:403
  10.6 3.2 copy.56
  13.8 0.0 copy-start
  13.9 2.1 reshape.108.anc
  16.0 0.0 copy-start.2
  16.0 0.0 copy-done
  16.0 0.8 copy.57
  16.8 1.4 reshape.106.rhs
  18.2 0.0 copy-done.2
  18.2 0.6 copy.45.pat
  18.8 0.0 all-to-all-done
  18.8 0.1 copy.49
  18.9 0.2 select_reduce_fusion
  19.1 0.2 select_reduce_fusion.1
  19.4 0.1 copy.40
  19.5 0.1 copy.41
  19.6 0.1 max.15
  19.7 0.6 stack.17.tab
  20.3 304.0 %shard_map.86 = (f32[4,32,8,128]{3,2,1,0:T(8,128)}, f32[32,8,8,128]{3,2,1,0:T(8,128)}) custom-call(s32[3,5,64]{2,1,0:T(8,128)} %stack.17.tab, s32[4,7,32]{2,1,0:T(8,128)} %copy.45.pat, f32[4,32,8,128]{3,2,1,0:T(8,128)} %reshape.106.rhs, f32[32,8,8,128]{3,2,1,0:T(8,128)} %reshape.108.anc, f32[4,32,16,128]{3,2,1,0:T(8,128)} %dinv.1, f32[4,8,32,16,128]{4,3,2,1,0:T(8,128)} %panels.1), custom_call_target="tpu_custom_call" | custom-call | flops 4000000000 | bytes 12000000 | tf_op jit(solution)/shard_map/pallas_call | solution.py:427
  324.3 2.7 reshape.111
  327.0 0.0 copy-start.1
  327.0 2.0 copy.47
  329.0 0.0 copy-done.1
  329.0 0.6 reshape.109
  329.6 1.3 copy.46
  (11 shorter events, 0.1 us)
Async XLA Ops:
  2.9 15.9 %all-to-all-start = ((s32[3,32,2]{0,2,1:T(2,128)}), s32[3,32,2]{0,2,1:T(2,128)S(1)}, u32[]{:S(2)}, u32[]{:S(2)}) async-start(s32[3,32,2]{0,2,1:T(2,128)} %bitcast), calls=%async_computation | async-start | bytes 65536 | tf_op jit(solution)/shard_map/all_to_all | solution.py:403
  13.8 2.1 copy-start
  16.0 2.2 copy-start.2
  327.0 2.0 copy-start.1

commit v2 on v1

--- a/solution.py
+++ b/solution.py
@@ -34,48 +34,27 @@
 
 
 def store_matrix(block):
-    wide = jnp.concatenate([block[:8], block[8:]], axis=1)
-    high, low = split(wide)
-    return jnp.concatenate([high, low], axis=0).astype(BF16)
-
-
-def expand(packed):
+    high, low = split(block)
+    return jnp.concatenate([high.astype(BF16), low.astype(BF16)], axis=1)
+
+
+def multiply(matrix, tiles):
     low = low_lanes((8, 128))
-    rolled = swap_halves(packed)
-    zero = jnp.zeros((8, 128), F32)
-    top, bottom = [], []
+    high, rest = split(tiles)
+    high_r, rest_r = swap_halves(high), swap_halves(rest)
+    rows = []
     for z in range(8):
-        top += [jnp.where(low, packed[z], zero), jnp.where(low, rolled[z], zero)]
-        bottom += [jnp.where(low, zero, rolled[z]), jnp.where(low, zero, packed[z])]
-    high, rest = split(jnp.concatenate(top + bottom, axis=0))
-    return jnp.concatenate([high.astype(BF16), rest.astype(BF16)], axis=1)
-
-
-def apply(matrix, weights):
-    o = jnp.dot(matrix, weights, preferred_element_type=F32).reshape(8, 2, 8, 256)
-    return o[:, 0, :, :128] + o[:, 0, :, 128:] + o[:, 1, :, :128]
-
-
-def apply_t(matrix, tiles):
-    count = tiles.shape[0]
-    high, rest = split(tiles)
-    zero = jnp.zeros((8, 128), F32)
-    rows = []
-    for d in range(count):
-        rows.append(jnp.concatenate([high[d], rest[d]], axis=1))
-        rows.append(jnp.concatenate([high[d], zero], axis=1))
+        rows += [jnp.where(low, high[z], rest_r[z]), jnp.where(low, high_r[z], rest[z])]
     weights = jnp.concatenate(rows, axis=0).astype(BF16)
-    o = lax.dot_general(matrix, weights, (((0,), (0,)), ((), ())), preferred_element_type=F32)
-    c = (o[:, :128] + o[:, 128:]).reshape(2, 8, 2, 8, 128)
+    weights = jnp.concatenate([weights, weights], axis=0)
+    o = jnp.dot(matrix, weights, preferred_element_type=F32).reshape(8, 2, 8, 128)
     low = low_lanes((8, 8, 128))
-    direct = jnp.where(low, c[0, :, 0], c[1, :, 1])
-    cross = jnp.where(low, c[0, :, 1], c[1, :, 0])
-    return direct + swap_halves(cross)
+    return jnp.where(low, o[:, 0], o[:, 1]) + swap_halves(jnp.where(low, o[:, 1], o[:, 0]))
 
 
 def kernel(
     ncol, tab, pat, rhs, anc, dinv, panels, sol_out, bu_out,
-    stage, ph, dv, dh, rsend, rs, sol, out, car, cum, fsend, frecv, bsend, brecv, anct,
+    stage, ph, pt, dv, dh, dt, rsend, rs, sol, out, car, cum, fsend, frecv, bsend, bulk, brecv, anct,
     part, rsr, tot, xsend, solr,
     sem_stage, sem_dv, sem_r, sem_ag_s, sem_ag_r, sem_fs, sem_fr, sem_bs, sem_br, sem_rs_s, sem_rs_r, sem_x,
 ):
@@ -100,15 +79,15 @@
         pl.semaphore_signal(barrier, inc=1, device_id={"col": lax.rem(col + k, ncol)}, device_id_type=pl.DeviceIdType.MESH)
 
     def load_panels(l):
-        return pltpu.make_async_copy(panels.at[l], stage.at[l % 2], sem_stage.at[l % 2])
+        place = (0, 0, 1, 1)[l]
+        return pltpu.make_async_copy(panels.at[l], stage.at[place], sem_stage.at[place])
 
     load_panels(0).start()
-    load_panels(1).start()
+    load_panels(3).start()
     pl.semaphore_wait(barrier, NR - 1 + ncol - 1)
 
     def row_send(src, dst, send_sem, recv_sem):
-        @pl.loop(1, NR)
-        def _(k):
+        for k in (4, 3, 5, 2, 6, 1, 7):
             z = lax.rem(row + k, NR)
             pltpu.make_async_remote_copy(
                 src_ref=src(z), dst_ref=dst(row), send_sem=send_sem, recv_sem=recv_sem,
@@ -127,16 +106,24 @@
         wait_bytes(dv.at[l, pl.ds(0, NR - 1)], sem_dv.at[1, l])
         wait_bytes(dv.at[l, 0], sem_dv.at[2, l])
         for j in range(OWN):
-            for z in range(NR):
-                dh[l, j, 16 * z : 16 * z + 16, :] = store_matrix(dv[l, z, j])
+            whole = dv[l, :, j].reshape(128, 128)
+            dh[l, j] = store_matrix(whole)
+            dt[l, j] = store_matrix(whole.T)
 
     def r_send(l):
         rs[l, row] = rsend[l, row]
-        row_send(lambda z: rsend.at[l, z], lambda o: rs.at[l, o], sem_r.at[0, l], sem_r.at[1, l])
-
-    def r_wait(l):
-        wait_bytes(rs.at[l, pl.ds(0, NR - 1)], sem_r.at[0, l])
-        wait_bytes(rs.at[l, pl.ds(0, NR - 1)], sem_r.at[1, l])
+        for h in range(2):
+            part_h = pl.ds(2 * h, 2)
+            row_send(
+                lambda z: rsend.at[l, z, part_h], lambda o: rs.at[l, o, part_h], sem_r.at[0, l, h], sem_r.at[1, l, h]
+            )
+
+    def r_wait(l, h):
+        wait_bytes(rs.at[l, pl.ds(0, NR - 1), pl.ds(2 * h, 2)], sem_r.at[1, l, h])
+
+    def r_wait_sent(l):
+        for h in range(2):
+            wait_bytes(rs.at[l, pl.ds(0, NR - 1), pl.ds(2 * h, 2)], sem_r.at[0, l, h])
 
     def col_send(src, dst, send_sem, recv_sem):
         @pl.loop(1, ncol)
@@ -154,7 +141,7 @@
 
     def fwd_pack_send(l, g):
         a, b = FWD_GROUPS[g]
-        src, dst = fsend[g], frecv[g].at[l]
+        src, dst = fsend[g], frecv[g].at[l % 2]
 
         @pl.loop(0, SLOTS, unroll=4)
         def _(s):
@@ -167,7 +154,7 @@
 
     def fwd_collect(l, g):
         a, b = FWD_GROUPS[g]
-        dst = frecv[g].at[l]
+        dst = frecv[g].at[l % 2]
         col_wait(dst, sem_fr.at[l, g])
         col_wait(fsend[g], sem_fs.at[l, g])
 
@@ -184,8 +171,12 @@
             def _(p):
                 car[p, pl.ds(a - 1, b - a)] = cum[tab[l, LAST, p], pl.ds(0, b - a)]
 
+    def bwd_buffer(l, g):
+        a, b = BWD_GROUPS[l][g]
+        return bulk.at[:, pl.ds(0, b - a)] if b - a > 1 else bsend.at[l, g]
+
     def bwd_pack_send(l, g, source):
-        src, dst = bsend[l][g], brecv[l][g]
+        src, dst = bwd_buffer(l, g), brecv[l][g]
 
         @pl.loop(0, SLOTS, unroll=4)
         def _(s):
@@ -196,7 +187,7 @@
         a, b = BWD_GROUPS[l][g]
         dst = brecv[l][g]
         col_wait(dst, sem_br.at[l, g])
-        col_wait(bsend[l][g], sem_bs.at[l, g])
+        col_wait(bwd_buffer(l, g), sem_bs.at[l, g])
 
         @pl.loop(0, SUP, unroll=4)
         def _(k):
@@ -207,13 +198,14 @@
 
         @pl.loop(0, SUP)
         def _(g):
-            for d in range(ANC):
-                block = stage[l % 2, d, g]
-                if d > 0:
-                    block = block * pat[l, d - 1, g].astype(F32)
-                ph[l, g, 16 * d : 16 * d + 16, :] = store_matrix(block)
-        if l + 2 < LEVELS:
-            load_panels(l + 2).start()
+            blocks = [stage[(0, 0, 1, 1)[l], 0, g]]
+            for d in range(1, ANC):
+                blocks.append(stage[(0, 0, 1, 1)[l], d, g] * pat[l, d - 1, g].astype(F32))
+            whole = jnp.concatenate(blocks, axis=0)
+            ph[l, g] = store_matrix(whole)
+            pt[l, g] = store_matrix(whole.T)
+        if l in (0, 3):
+            load_panels((1, None, None, 2)[l]).start()
 
     def ag_copy(l, c, t, way):
         origin = at_row(1 - t) if way == 0 else at_row(t - 1)
@@ -227,18 +219,19 @@
         return (0, 1) if t < 4 else (c % 2,)
 
     def product(l, g):
-        out[g] = apply(ph[l, g], expand(sol[l, g // OWN, g % OWN].reshape(8, 8, 128)))
+        out[g] = multiply(ph[l, g], sol[l, g // OWN, g % OWN].reshape(8, 8, 128))
 
     def solve(l):
-        r_wait(l)
-        for c in range(OWN):
-            sol[l, row, c] = apply(dh[l, c], expand(rs[l, :, c])).reshape(64, 128)
+        for c in range(OWN):
+            if c % 2 == 0:
+                r_wait(l, c // 2)
+            sol[l, row, c] = multiply(dh[l, c], rs[l, :, c]).reshape(64, 128)
             for way in ag_ways(c, 1):
                 ag_copy(l, c, 1, way).start()
-
-    def spread_solved(l):
-        @pl.loop(0, OWN)
-        def _(c):
+        r_wait_sent(l)
+
+    def spread_solved(l, extra=None):
+        for c in range(OWN):
             product(l, row * OWN + c)
         for t in range(1, 5):
             for c in range(OWN):
@@ -249,9 +242,10 @@
                 if t == 4:
                     product(l, at_row(4) * OWN + c)
                 else:
-                    @pl.loop(0, 2)
-                    def _(w):
-                        product(l, lax.rem(row + NR - t + 2 * t * w, NR) * OWN + c)
+                    for offset in (-t, t):
+                        product(l, at_row(offset) * OWN + c)
+            if extra is not None:
+                extra(t)
         for t in range(1, 5):
             for c in range(OWN):
                 for way in ag_ways(c, t):
@@ -265,48 +259,60 @@
 
     def rs_copy(l, c, t, way):
         first = t == 1 or way not in rs_ways(c, t - 1)
-        src = part.at[rs_dest(t, way), c] if first else rsr.at[l, way, t - 2, c]
+        src = part.at[rs_dest(t, way), c] if first else rsr.at[l % 2, way, t - 2, c]
         return pltpu.make_async_remote_copy(
-            src_ref=src, dst_ref=rsr.at[l, way, t - 1, c],
+            src_ref=src, dst_ref=rsr.at[l % 2, way, t - 1, c],
             send_sem=sem_rs_s.at[l, c, t - 1, way], recv_sem=sem_rs_r.at[l, c, t - 1, way],
             device_id=rowdev(right if way == 0 else left), device_id_type=pl.DeviceIdType.MESH,
         )
 
-    def sum_over_row(l, make):
-        for t in range(1, 5):
-            if t == 1:
-                for c in range(OWN):
-                    make(at_row(4) * OWN + c)
-            else:
-                for c in range(OWN):
-                    @pl.loop(0, 2)
-                    def _(w):
-                        make(lax.rem(row + NR + (5 - t) * (1 - 2 * w), NR) * OWN + c)
-            for c in range(OWN):
-                for way in rs_ways(c, t):
-                    if t > 1 and way in rs_ways(c, t - 1):
-                        rs_copy(l, c, t - 1, way).wait_recv()
-                        rsr[l, way, t - 2, c] += part[rs_dest(t, way), c]
-                    rs_copy(l, c, t, way).start()
-        for c in range(OWN):
-            make(row * OWN + c)
+    def ring_step(l, t):
+        for c in range(OWN):
+            for way in rs_ways(c, t):
+                if t > 1 and way in rs_ways(c, t - 1):
+                    rs_copy(l, c, t - 1, way).wait_recv()
+                    rsr[l % 2, way, t - 2, c] += part[rs_dest(t, way), c]
+                rs_copy(l, c, t, way).start()
+
+    def ring_end(l, done):
         for c in range(OWN):
             for way in (0, 1):
                 rs_copy(l, c, 4, way).wait_recv()
-            tot[l, c] = part[row, c] + rsr[l, 0, 3, c] + rsr[l, 1, 3, c]
+            total = part[row, c] + rsr[l % 2, 0, 3, c] + rsr[l % 2, 1, 3, c]
+            done(c, total)
         for c in range(OWN):
             for t in range(1, 5):
                 for way in rs_ways(c, t):
                     rs_copy(l, c, t, way).wait_send()
 
-    def finish(l):
-        for c in range(OWN):
-            reduced = (sol[l, row, c] - tot[l, c]).reshape(8, 8, 128)
-            xsend[l, :, c] = apply_t(dh[l, c], reduced)
-        solr[l, row] = xsend[l, row]
-        row_send(lambda z: xsend.at[l, z], lambda o: solr.at[l, o], sem_x.at[0, l], sem_x.at[1, l])
-        wait_bytes(solr.at[l, pl.ds(0, NR - 1)], sem_x.at[1, l])
-        wait_bytes(solr.at[l, pl.ds(0, NR - 1)], sem_x.at[0, l])
+    def sum_over_row(l, make, done):
+        for t in range(1, 5):
+            for offset in (4,) if t == 1 else (5 - t, t - 5):
+                for c in range(OWN):
+                    make(at_row(offset) * OWN + c)
+            ring_step(l, t)
+        for c in range(OWN):
+            make(row * OWN + c)
+        ring_end(l, done)
+
+    def keep(c, total):
+        tot[c] = total
+
+    def finish(l, c, total):
+        reduced = (sol[l, row, c] - total).reshape(8, 8, 128)
+        xsend[l, :, c] = multiply(dt[l, c], reduced)
+        if c % 2 == 1:
+            h = c // 2
+            part_h = pl.ds(2 * h, 2)
+            solr[l, row, part_h] = xsend[l, row, part_h]
+            row_send(
+                lambda z: xsend.at[l, z, part_h], lambda o: solr.at[l, o, part_h], sem_x.at[0, l, h], sem_x.at[1, l, h]
+            )
+
+    def finish_wait(l):
+        for h in range(2):
+            for k in (1, 0):
+                wait_bytes(solr.at[l, pl.ds(0, NR - 1), pl.ds(2 * h, 2)], sem_x.at[k, l, h])
 
     def emit(l):
         sol_out[l] = solr[l].reshape(SUP, 8, 128)
@@ -314,20 +320,27 @@
     def set_part(g, value):
         part[g // OWN, g % OWN] = value.reshape(64, 128)
 
-    for l in range(LEVELS):
-        dinv_send(l)
+    def top_part(t):
+        @pl.loop(8 * t - 8, 8 * t, unroll=2)
+        def _(g):
+            set_part(g, multiply(pt[3, g], anc[g]))
+
     rsend[0] = rhs[0].reshape(NR, OWN, 8, 128)
     r_send(0)
+    dinv_send(0)
     cum[SLOTS] = jnp.zeros(cum.shape[1:], F32)
     bwd_pack_send(2, 1, lambda k: anc[k, pl.ds(0, 7)])
     convert(0)
+    convert(3)
     dinv_wait(0)
     for l in range(LEVELS - 1):
         solve(l)
-        spread_solved(l)
+        spread_solved(l, top_part if l == 0 else None)
         if l > 0:
             fwd_collect(l - 1, 1)
         fwd_pack_send(l, 0)
+        dinv_send(l + 1)
+        ring_step(3, (1, 3, 4)[l])
         if l > 0:
             fwd_collect(l - 1, 2)
 
@@ -336,7 +349,12 @@
                 car[g, 7] = jnp.zeros((8, 128), F32)
         fwd_pack_send(l, 1)
         fwd_pack_send(l, 2)
-        convert(l + 1)
+        if l + 1 < 3:
+            convert(l + 1)
+        if l == 0:
+            ring_step(3, 2)
+        fwd_collect(l, 0)
+        r_send(l + 1)
         dinv_wait(l + 1)
         if l == 0:
             bwd_gather(2, 1)
@@ -344,13 +362,12 @@
         if l == 1:
             bwd_gather(1, 2)
             bwd_pack_send(0, 3, lambda k: anct[1, k, pl.ds(2, 5)])
-        if l == 2:
-            sum_over_row(3, lambda g: set_part(g, apply_t(ph[3, g], anc[g])))
-        fwd_collect(l, 0)
-        r_send(l + 1)
-
+
+    ring_end(3, keep)
     solve(3)
-    finish(3)
+    for c in range(OWN):
+        finish(3, c, tot[c])
+    finish_wait(3)
     bwd_pack_send(2, 0, lambda k: solr[3, k // OWN, pl.ds(k % OWN, 1)])
     emit(3)
     spread_solved(3)
@@ -369,10 +386,6 @@
             bwd_gather(0, 3)
             bwd_gather(0, 2)
             bwd_gather(0, 1)
-
-        @pl.loop(0, SUP)
-        def _(g):
-            set_part(g, apply_t(ph[l, g, 16:, :], anct[l, g, pl.ds(1, 7)]))
         bwd_gather(l, 0)
         if l == 2:
             bwd_pack_send(1, 1, lambda k: anct[2, k, pl.ds(0, 1)])
@@ -380,11 +393,10 @@
             bwd_pack_send(0, 1, lambda k: anct[1, k, pl.ds(0, 1)])
             bwd_pack_send(0, 2, lambda k: anct[1, k, pl.ds(1, 1)])
 
-        def add_part(g):
-            extra = apply_t(ph[l, g, 0:16, :], anct[l, g, pl.ds(0, 1)])
-            part[g // OWN, g % OWN] += extra.reshape(64, 128)
-        sum_over_row(l, add_part)
-        finish(l)
+        sum_over_row(
+            l, lambda g: set_part(g, multiply(pt[l, g], anct[l, g])), functools.partial(finish, l)
+        )
+        finish_wait(l)
         if l > 0:
             bwd_pack_send(l - 1, 0, lambda k: solr[l, k // OWN, pl.ds(k % OWN, 1)])
         emit(l)
@@ -422,7 +434,7 @@
     sems = pltpu.SemaphoreType.DMA
     tile = (8, 128)
     fsend = tuple(pltpu.VMEM((SLOTS, b - a) + tile, F32) for a, b in FWD_GROUPS)
-    frecv = tuple(pltpu.VMEM((3, SLOTS, b - a) + tile, F32) for a, b in FWD_GROUPS)
+    frecv = tuple(pltpu.VMEM((2, SLOTS, b - a) + tile, F32) for a, b in FWD_GROUPS)
     bbuf = tuple(tuple(pltpu.VMEM((SLOTS, b - a) + tile, F32) for a, b in groups) for groups in BWD_GROUPS)
     sol, bu = pl.pallas_call(
         functools.partial(kernel, ncol),
@@ -435,7 +447,9 @@
         scratch_shapes=[
             pltpu.VMEM((2, ANC, SUP, 16, 128), F32),
             pltpu.VMEM((LEVELS, SUP, 128, 256), BF16),
+            pltpu.VMEM((LEVELS, SUP, 128, 256), BF16),
             pltpu.VMEM((LEVELS, NR, OWN, 16, 128), F32),
+            pltpu.VMEM((LEVELS, OWN, 128, 256), BF16),
             pltpu.VMEM((LEVELS, OWN, 128, 256), BF16),
             pltpu.VMEM((LEVELS, NR, OWN) + tile, F32),
             pltpu.VMEM((LEVELS, NR, OWN) + tile, F32),
@@ -443,17 +457,17 @@
             pltpu.VMEM((SUP, ANC) + tile, F32),
             pltpu.VMEM((SUP, ANC) + tile, F32),
             pltpu.VMEM((SLOTS + 1, 6) + tile, F32),
-            fsend, frecv, bbuf, bbuf,
+            fsend, frecv, pltpu.VMEM((3, 3, SLOTS, 1) + tile, F32), pltpu.VMEM((SLOTS, 7) + tile, F32), bbuf,
             pltpu.VMEM((3, SUP, ANC) + tile, F32),
             pltpu.VMEM((NR, OWN, 64, 128), F32),
-            pltpu.VMEM((LEVELS, 2, 4, OWN, 64, 128), F32),
-            pltpu.VMEM((LEVELS, OWN, 64, 128), F32),
+            pltpu.VMEM((2, 2, 4, OWN, 64, 128), F32),
+            pltpu.VMEM((OWN, 64, 128), F32),
             pltpu.VMEM((LEVELS, NR, OWN) + tile, F32),
             pltpu.VMEM((LEVELS, NR, OWN) + tile, F32),
-            sems((2,)), sems((3, LEVELS)), sems((2, LEVELS)),
+            sems((2,)), sems((3, LEVELS)), sems((2, LEVELS, 2)),
             sems((LEVELS, OWN, 4, 2)), sems((LEVELS, OWN, 4, 2)),
             sems((3, 3)), sems((3, 3)), sems((3, 4)), sems((3, 4)),
-            sems((LEVELS, OWN, 4, 2)), sems((LEVELS, OWN, 4, 2)), sems((2, LEVELS)),
+            sems((LEVELS, OWN, 4, 2)), sems((LEVELS, OWN, 4, 2)), sems((2, LEVELS, 2)),
         ],
         compiler_params=pltpu.CompilerParams(
             collective_id=0, has_side_effects=True, vmem_limit_bytes=60 * 1024 * 1024

time: 331 us -> 286 us (0.86)
  Pallas kernels: 304 us -> 257 us
    pallas_call x1, Pallas kernels: 304 us -> 257 us  [per_device(): pl.pallas_call(functools.partial(kernel, ncol), out_shape=(jax.ShapeDtype...]
  transfers between devices with their start and end apart: 1 -> 1, of which waited for: 0 -> 0; matrix products, arithmetic and copies ran while one was open for 2% -> 3% of each run, Pallas kernels for 0% -> 0%
where the time goes in v2:
time: 286 us; the launch traced here: 284 us
  Pallas kernels  257 us (90%)
  local copies, waits for them, and re-layouts  16.9 us (6%)
  starting transfers between devices  7.62 us (3%)
    pallas_call x1, Pallas kernels, per_device(): pl.pallas_call(functools.partial(kernel, ncol), out_shape=(jax.ShapeDtype...  257 us
    all_to_all x1, starting transfers between devices, tables(): lax.all_to_all(ids.reshape(3, ncol, cap), 'col', split_axis=1, concat_axi...  7.62 us
  transfers between devices with their start and end apart: 1, of which 0 were waited for; matrix products, arithmetic and copies ran while one was open for 3% of the time, Pallas kernels for 0%

profile of v2, /device:TPU:2, one launch (start us, length us, event | category | flops | bytes accessed | tf_op | source)
XLA Modules:
  0.0 283.8 jit_solution(1739890322742696761)
XLA Ops:
  0.6 0.7 copy.58
  1.3 0.1 convert_reduce_fusion
  1.4 0.7 multiply_add_fusion
  2.1 0.1 select_reduce_fusion.2
  2.2 0.7 copy.48
  2.9 7.6 %all-to-all-start = ((s32[3,32,2]{0,2,1:T(2,128)}), s32[3,32,2]{0,2,1:T(2,128)S(1)}, u32[]{:S(2)}, u32[]{:S(2)}) async-start(s32[3,32,2]{0,2,1:T(2,128)} %bitcast), calls=%async_computation | async-start | bytes 65536 | tf_op jit(solution)/shard_map/all_to_all | solution.py:415
  10.6 3.2 %copy.56 = f32[2,8,32,8,64]{4,0,1,3,2:T(2,128)S(1)} copy(f32[2,8,32,8,64]{4,3,2,1,0:T(8,128)} %bitcast.27) | data formatting | bytes 2097152 | tf_op jit(solution)/shard_map/reshape | solution.py:430
  13.8 0.0 copy-start
  13.9 2.1 reshape.108.anc
  16.0 0.0 copy-start.2
  16.0 0.0 copy-done
  16.0 0.8 copy.57
  16.8 1.4 reshape.106.rhs
  18.2 0.0 copy-done.2
  18.2 0.6 copy.45.pat
  18.8 0.0 all-to-all-done
  18.8 0.1 copy.49
  18.9 0.2 select_reduce_fusion
  19.1 0.2 select_reduce_fusion.1
  19.4 0.1 copy.40
  19.5 0.1 copy.41
  19.6 0.1 max.15
  19.7 0.6 stack.17.tab
  20.3 257.1 %shard_map.86 = (f32[4,32,8,128]{3,2,1,0:T(8,128)}, f32[32,8,8,128]{3,2,1,0:T(8,128)}) custom-call(s32[3,5,64]{2,1,0:T(8,128)} %stack.17.tab, s32[4,7,32]{2,1,0:T(8,128)} %copy.45.pat, f32[4,32,8,128]{3,2,1,0:T(8,128)} %reshape.106.rhs, f32[32,8,8,128]{3,2,1,0:T(8,128)} %reshape.108.anc, f32[4,32,16,128]{3,2,1,0:T(8,128)} %dinv.1, f32[4,8,32,16,128]{4,3,2,1,0:T(8,128)} %panels.1), custom_call_target="tpu_custom_call" | custom-call | flops 4000000000 | bytes 12000000 | tf_op jit(solution)/shard_map/pallas_call | solution.py:439
  277.4 2.5 reshape.111
  279.9 0.0 copy-start.1
  279.9 2.0 copy.47
  281.9 0.0 copy-done.1
  281.9 0.6 reshape.109
  282.5 1.3 copy.46
  (11 shorter events, 0.1 us)
Async XLA Ops:
  2.9 15.9 %all-to-all-start = ((s32[3,32,2]{0,2,1:T(2,128)}), s32[3,32,2]{0,2,1:T(2,128)S(1)}, u32[]{:S(2)}, u32[]{:S(2)}) async-start(s32[3,32,2]{0,2,1:T(2,128)} %bitcast), calls=%async_computation | async-start | bytes 65536 | tf_op jit(solution)/shard_map/all_to_all | solution.py:415
  13.8 2.1 copy-start
  16.0 2.2 copy-start.2
  279.9 2.0 copy-start.1

commit v3 on v2

--- a/solution.py
+++ b/solution.py
@@ -54,9 +54,9 @@
 
 def kernel(
     ncol, tab, pat, rhs, anc, dinv, panels, sol_out, bu_out,
-    stage, ph, pt, dv, dh, dt, rsend, rs, sol, out, car, cum, fsend, frecv, bsend, bulk, brecv, anct,
+    stage, ph, pt, dv, dh, dt, pv, p0, rsend, rs, asend, ar, own, sol, out, car, cum, fsend, frecv, bsend, bulk, brecv, anct,
     part, rsr, tot, xsend, solr,
-    sem_stage, sem_dv, sem_r, sem_ag_s, sem_ag_r, sem_fs, sem_fr, sem_bs, sem_br, sem_rs_s, sem_rs_r, sem_x,
+    sem_stage, sem_dv, sem_p, sem_a, sem_r, sem_ag_s, sem_ag_r, sem_fs, sem_fr, sem_bs, sem_br, sem_rs_s, sem_rs_r, sem_x,
 ):
     row, col = lax.axis_index("row"), lax.axis_index("col")
     cap = SLOTS // ncol
@@ -110,6 +110,31 @@
             dh[l, j] = store_matrix(whole)
             dt[l, j] = store_matrix(whole.T)
 
+    def p0_send(l):
+        row_send(lambda z: panels.at[l, 0, pl.ds(z * OWN, OWN)], lambda o: pv.at[l, o], sem_p.at[0, l], sem_p.at[1, l])
+        pltpu.make_async_copy(panels.at[l, 0, pl.ds(row * OWN, OWN)], pv.at[l, row], sem_p.at[2, l]).start()
+
+    def p0_wait(l):
+        wait_bytes(pv.at[l, pl.ds(0, NR - 1)], sem_p.at[0, l])
+        wait_bytes(pv.at[l, pl.ds(0, NR - 1)], sem_p.at[1, l])
+        wait_bytes(pv.at[l, 0], sem_p.at[2, l])
+        for j in range(OWN):
+            p0[l, j] = store_matrix(pv[l, :, j].reshape(128, 128).T)
+
+    def a_send(l):
+        col_wait(brecv[l][0], sem_br.at[l, 0])
+        col_wait(bwd_buffer(l, 0), sem_bs.at[l, 0])
+
+        @pl.loop(0, SUP, unroll=4)
+        def _(k):
+            asend[l, k // OWN, k % OWN] = brecv[l][0][tab[l, POS, k], 0]
+        ar[l, row] = asend[l, row]
+        row_send(lambda z: asend.at[l, z], lambda o: ar.at[l, o], sem_a.at[0, l], sem_a.at[1, l])
+
+    def a_wait(l):
+        wait_bytes(ar.at[l, pl.ds(0, NR - 1)], sem_a.at[1, l])
+        wait_bytes(ar.at[l, pl.ds(0, NR - 1)], sem_a.at[0, l])
+
     def r_send(l):
         rs[l, row] = rsend[l, row]
         for h in range(2):
@@ -125,16 +150,29 @@
         for h in range(2):
             wait_bytes(rs.at[l, pl.ds(0, NR - 1), pl.ds(2 * h, 2)], sem_r.at[0, l, h])
 
-    def col_send(src, dst, send_sem, recv_sem):
-        @pl.loop(1, ncol)
-        def _(k):
+    def col_send(src, dst, send_sem, recv_sem, pack):
+        for i in range(cap):
+            pack(src, dst, col * cap + i)
+        dst[pl.ds(col * cap, cap)] = src[pl.ds(col * cap, cap)]
+
+        def one(k):
             c = lax.rem(col + k, ncol)
+            for i in range(cap):
+                pack(src, dst, c * cap + i)
             pltpu.make_async_remote_copy(
                 src_ref=src.at[pl.ds(c * cap, cap)], dst_ref=dst.at[pl.ds(col * cap, cap)],
                 send_sem=send_sem, recv_sem=recv_sem,
                 device_id={"col": c}, device_id_type=pl.DeviceIdType.MESH,
             ).start()
-        dst[pl.ds(col * cap, cap)] = src[pl.ds(col * cap, cap)]
+
+        steps = (ncol - 1) // 3
+
+        @pl.loop(0, steps)
+        def _(k):
+            for i in range(3):
+                one(3 * k + i + 1)
+        for k in range(3 * steps + 1, ncol):
+            one(k)
 
     def col_wait(dst, sem):
         wait_bytes(dst.at[pl.ds(0, SLOTS - cap)], sem)
@@ -143,14 +181,13 @@
         a, b = FWD_GROUPS[g]
         src, dst = fsend[g], frecv[g].at[l % 2]
 
-        @pl.loop(0, SLOTS, unroll=4)
-        def _(s):
+        def pack(src, dst, s):
             k = tab[l, FSRC, s]
-            if l == 0 or a == 7:
+            if l == 0:
                 src[s] = out[k, pl.ds(a, b - a)]
             else:
                 src[s] = out[k, pl.ds(a, b - a)] + car[k, pl.ds(a, b - a)]
-        col_send(src, dst, sem_fs.at[l, g], sem_fr.at[l, g])
+        col_send(src, dst, sem_fs.at[l, g], sem_fr.at[l, g], pack)
 
     def fwd_collect(l, g):
         a, b = FWD_GROUPS[g]
@@ -178,10 +215,9 @@
     def bwd_pack_send(l, g, source):
         src, dst = bwd_buffer(l, g), brecv[l][g]
 
-        @pl.loop(0, SLOTS, unroll=4)
-        def _(s):
+        def pack(src, dst, s):
             src[s] = source(tab[l, BSRC, s])
-        col_send(src, dst, sem_bs.at[l, g], sem_br.at[l, g])
+        col_send(src, dst, sem_bs.at[l, g], sem_br.at[l, g], pack)
 
     def bwd_gather(l, g):
         a, b = BWD_GROUPS[l][g]
@@ -193,24 +229,26 @@
         def _(k):
             anct[l, k, pl.ds(a, b - a)] = dst[tab[l, POS, k]]
 
-    def convert(l):
-        load_panels(l).wait()
-
-        @pl.loop(0, SUP)
+    def convert(l, low=0, high=SUP):
+        place = (0, 0, 1, 1)[l]
+        if low == 0:
+            load_panels(l).wait()
+
+        @pl.loop(low, high)
         def _(g):
-            blocks = [stage[(0, 0, 1, 1)[l], 0, g]]
+            blocks = [stage[place, 0, g]]
             for d in range(1, ANC):
-                blocks.append(stage[(0, 0, 1, 1)[l], d, g] * pat[l, d - 1, g].astype(F32))
+                blocks.append(stage[place, d, g] * pat[l, d - 1, g].astype(F32))
             whole = jnp.concatenate(blocks, axis=0)
             ph[l, g] = store_matrix(whole)
             pt[l, g] = store_matrix(whole.T)
-        if l in (0, 3):
+        if l in (0, 3) and high == SUP:
             load_panels((1, None, None, 2)[l]).start()
 
     def ag_copy(l, c, t, way):
         origin = at_row(1 - t) if way == 0 else at_row(t - 1)
         return pltpu.make_async_remote_copy(
-            src_ref=sol.at[l, origin, c], dst_ref=sol.at[l, origin, c],
+            src_ref=sol.at[l % 2, origin, c], dst_ref=sol.at[l % 2, origin, c],
             send_sem=sem_ag_s.at[l, c, t - 1, way], recv_sem=sem_ag_r.at[l, c, t - 1, way],
             device_id=rowdev(right if way == 0 else left), device_id_type=pl.DeviceIdType.MESH,
         )
@@ -219,37 +257,41 @@
         return (0, 1) if t < 4 else (c % 2,)
 
     def product(l, g):
-        out[g] = multiply(ph[l, g], sol[l, g // OWN, g % OWN].reshape(8, 8, 128))
+        out[g] = multiply(ph[l, g], sol[l % 2, g // OWN, g % OWN].reshape(8, 8, 128))
 
     def solve(l):
         for c in range(OWN):
             if c % 2 == 0:
                 r_wait(l, c // 2)
-            sol[l, row, c] = multiply(dh[l, c], rs[l, :, c]).reshape(64, 128)
+            own[l, c] = multiply(dh[l, c], rs[l, :, c]).reshape(64, 128)
+            sol[l % 2, row, c] = own[l, c]
             for way in ag_ways(c, 1):
                 ag_copy(l, c, 1, way).start()
         r_wait_sent(l)
 
+    def spread_step(l, t):
+        if t == 0:
+            for c in range(OWN):
+                product(l, row * OWN + c)
+            return
+        for c in range(OWN):
+            for way in ag_ways(c, t):
+                ag_copy(l, c, t, way).wait_recv()
+                if t < 4 and way in ag_ways(c, t + 1):
+                    ag_copy(l, c, t + 1, way).start()
+            for offset in (4,) if t == 4 else (-t, t):
+                product(l, at_row(offset) * OWN + c)
+        if t == 4:
+            for t in range(1, 5):
+                for c in range(OWN):
+                    for way in ag_ways(c, t):
+                        ag_copy(l, c, t, way).wait_send()
+
     def spread_solved(l, extra=None):
-        for c in range(OWN):
-            product(l, row * OWN + c)
-        for t in range(1, 5):
-            for c in range(OWN):
-                for way in ag_ways(c, t):
-                    ag_copy(l, c, t, way).wait_recv()
-                    if t < 4 and way in ag_ways(c, t + 1):
-                        ag_copy(l, c, t + 1, way).start()
-                if t == 4:
-                    product(l, at_row(4) * OWN + c)
-                else:
-                    for offset in (-t, t):
-                        product(l, at_row(offset) * OWN + c)
-            if extra is not None:
+        for t in range(5):
+            spread_step(l, t)
+            if extra is not None and t < 4:
                 extra(t)
-        for t in range(1, 5):
-            for c in range(OWN):
-                for way in ag_ways(c, t):
-                    ag_copy(l, c, t, way).wait_send()
 
     def rs_dest(t, way):
         return at_row(5 - t) if way == 0 else at_row(t - 5)
@@ -259,7 +301,7 @@
 
     def rs_copy(l, c, t, way):
         first = t == 1 or way not in rs_ways(c, t - 1)
-        src = part.at[rs_dest(t, way), c] if first else rsr.at[l % 2, way, t - 2, c]
+        src = part.at[l % 2, rs_dest(t, way), c] if first else rsr.at[l % 2, way, t - 2, c]
         return pltpu.make_async_remote_copy(
             src_ref=src, dst_ref=rsr.at[l % 2, way, t - 1, c],
             send_sem=sem_rs_s.at[l, c, t - 1, way], recv_sem=sem_rs_r.at[l, c, t - 1, way],
@@ -271,35 +313,28 @@
             for way in rs_ways(c, t):
                 if t > 1 and way in rs_ways(c, t - 1):
                     rs_copy(l, c, t - 1, way).wait_recv()
-                    rsr[l % 2, way, t - 2, c] += part[rs_dest(t, way), c]
+                    rsr[l % 2, way, t - 2, c] += part[l % 2, rs_dest(t, way), c]
                 rs_copy(l, c, t, way).start()
 
-    def ring_end(l, done):
+    def ring_end(l):
         for c in range(OWN):
             for way in (0, 1):
                 rs_copy(l, c, 4, way).wait_recv()
-            total = part[row, c] + rsr[l % 2, 0, 3, c] + rsr[l % 2, 1, 3, c]
-            done(c, total)
+            tot[c] = part[l % 2, row, c] + rsr[l % 2, 0, 3, c] + rsr[l % 2, 1, 3, c]
         for c in range(OWN):
             for t in range(1, 5):
                 for way in rs_ways(c, t):
                     rs_copy(l, c, t, way).wait_send()
 
-    def sum_over_row(l, make, done):
-        for t in range(1, 5):
-            for offset in (4,) if t == 1 else (5 - t, t - 5):
-                for c in range(OWN):
-                    make(at_row(offset) * OWN + c)
-            ring_step(l, t)
-        for c in range(OWN):
-            make(row * OWN + c)
-        ring_end(l, done)
-
-    def keep(c, total):
-        tot[c] = total
-
-    def finish(l, c, total):
-        reduced = (sol[l, row, c] - total).reshape(8, 8, 128)
+    def partial_sums(l, low, high):
+        @pl.loop(low, high, unroll=2)
+        def _(g):
+            part[l % 2, g // OWN, g % OWN] = multiply(pt[l, g], anc[g] if l == 3 else anct[l, g]).reshape(64, 128)
+
+    def finish(l, c):
+        reduced = (own[l, c] - tot[c]).reshape(8, 8, 128)
+        if l < 3:
+            reduced = reduced - multiply(p0[l, c], ar[l, :, c])
         xsend[l, :, c] = multiply(dt[l, c], reduced)
         if c % 2 == 1:
             h = c // 2
@@ -317,60 +352,122 @@
     def emit(l):
         sol_out[l] = solr[l].reshape(SUP, 8, 128)
 
-    def set_part(g, value):
-        part[g // OWN, g % OWN] = value.reshape(64, 128)
-
-    def top_part(t):
-        @pl.loop(8 * t - 8, 8 * t, unroll=2)
-        def _(g):
-            set_part(g, multiply(pt[3, g], anc[g]))
+    def finish_all(l):
+        for c in range(OWN):
+            finish(l, c)
+
+    def send_down(l):
+        bwd_pack_send(l, 0, lambda k: solr[l + 1, k // OWN, pl.ds(k % OWN, 1)])
+
+    def beside(l, t):
+        if l == 0:
+            if t < 2:
+                convert(1, 16 * t, 16 * t + 16)
+            else:
+                partial_sums(3, 16 * t - 32, 16 * t - 16)
+        elif l == 1:
+            if t < 2:
+                convert(2, 16 * t, 16 * t + 16)
+            elif t == 2:
+                ring_step(3, 2)
+                bwd_gather(2, 1)
+                bwd_pack_send(1, 2, lambda k: anct[2, k, pl.ds(1, 6)])
+            else:
+                fwd_collect(0, 1)
+                fwd_collect(0, 2)
+        else:
+            if t < 2:
+                partial_sums(2, 16 * t, 16 * t + 16)
+            elif t == 2:
+                bwd_gather(1, 2)
+                bwd_pack_send(0, 3, lambda k: anct[1, k, pl.ds(2, 5)])
+            else:
+                fwd_collect(1, 1)
+                fwd_collect(1, 2)
 
     rsend[0] = rhs[0].reshape(NR, OWN, 8, 128)
     r_send(0)
     dinv_send(0)
     cum[SLOTS] = jnp.zeros(cum.shape[1:], F32)
     bwd_pack_send(2, 1, lambda k: anc[k, pl.ds(0, 7)])
+
+    @pl.loop(0, SUP)
+    def _(g):
+        car[g, 7] = jnp.zeros((8, 128), F32)
+        for l in range(3):
+            anct[l, g, 0] = jnp.zeros((8, 128), F32)
     convert(0)
     convert(3)
     dinv_wait(0)
     for l in range(LEVELS - 1):
         solve(l)
-        spread_solved(l, top_part if l == 0 else None)
-        if l > 0:
-            fwd_collect(l - 1, 1)
+        spread_solved(l, functools.partial(beside, l))
         fwd_pack_send(l, 0)
         dinv_send(l + 1)
         ring_step(3, (1, 3, 4)[l])
-        if l > 0:
-            fwd_collect(l - 1, 2)
-
-            @pl.loop(0, SUP)
-            def _(g):
-                car[g, 7] = jnp.zeros((8, 128), F32)
         fwd_pack_send(l, 1)
-        fwd_pack_send(l, 2)
-        if l + 1 < 3:
-            convert(l + 1)
-        if l == 0:
-            ring_step(3, 2)
         fwd_collect(l, 0)
         r_send(l + 1)
+        p0_send(l)
+        fwd_pack_send(l, 2)
         dinv_wait(l + 1)
-        if l == 0:
-            bwd_gather(2, 1)
-            bwd_pack_send(1, 2, lambda k: anct[2, k, pl.ds(1, 6)])
-        if l == 1:
-            bwd_gather(1, 2)
-            bwd_pack_send(0, 3, lambda k: anct[1, k, pl.ds(2, 5)])
-
-    ring_end(3, keep)
+
+    ring_step(2, 1)
+    ring_end(3)
     solve(3)
-    for c in range(OWN):
-        finish(3, c, tot[c])
+    finish_all(3)
+    ring_step(2, 2)
+    ring_step(2, 3)
+    p0_wait(2)
     finish_wait(3)
-    bwd_pack_send(2, 0, lambda k: solr[3, k // OWN, pl.ds(k % OWN, 1)])
+    send_down(2)
+    spread_step(3, 0)
+    ring_step(2, 4)
+    p0_wait(1)
     emit(3)
-    spread_solved(3)
+    spread_step(3, 1)
+
+    a_send(2)
+    bwd_pack_send(1, 1, lambda k: asend[2, k // OWN, pl.ds(k % OWN, 1)])
+    ring_end(2)
+    spread_step(3, 2)
+    a_wait(2)
+    finish_all(2)
+    p0_wait(0)
+    bwd_gather(1, 1)
+    partial_sums(1, 0, SUP)
+    ring_step(1, 1)
+    finish_wait(2)
+    send_down(1)
+    ring_step(1, 2)
+    emit(2)
+    ring_step(1, 3)
+
+    a_send(1)
+    bwd_pack_send(0, 1, lambda k: asend[1, k // OWN, pl.ds(k % OWN, 1)])
+    bwd_pack_send(0, 2, lambda k: anct[1, k, pl.ds(1, 1)])
+    ring_step(1, 4)
+    bwd_gather(0, 3)
+    ring_end(1)
+    a_wait(1)
+    finish_all(1)
+    bwd_gather(0, 2)
+    bwd_gather(0, 1)
+    partial_sums(0, 0, SUP)
+    ring_step(0, 1)
+    finish_wait(1)
+    send_down(0)
+    ring_step(0, 2)
+    emit(1)
+    ring_step(0, 3)
+
+    a_send(0)
+    ring_step(0, 4)
+    spread_step(3, 3)
+    ring_end(0)
+    a_wait(0)
+    finish_all(0)
+    spread_step(3, 4)
     fwd_collect(2, 1)
     fwd_collect(2, 2)
 
@@ -378,28 +475,8 @@
     def _(g):
         bu_out[g, pl.ds(0, 7)] = out[g, pl.ds(0, 7)] + car[g, pl.ds(0, 7)]
         bu_out[g, 7] = out[g, 7]
-
-    for l in (2, 1, 0):
-        if l == 1:
-            bwd_gather(1, 1)
-        if l == 0:
-            bwd_gather(0, 3)
-            bwd_gather(0, 2)
-            bwd_gather(0, 1)
-        bwd_gather(l, 0)
-        if l == 2:
-            bwd_pack_send(1, 1, lambda k: anct[2, k, pl.ds(0, 1)])
-        if l == 1:
-            bwd_pack_send(0, 1, lambda k: anct[1, k, pl.ds(0, 1)])
-            bwd_pack_send(0, 2, lambda k: anct[1, k, pl.ds(1, 1)])
-
-        sum_over_row(
-            l, lambda g: set_part(g, multiply(pt[l, g], anct[l, g])), functools.partial(finish, l)
-        )
-        finish_wait(l)
-        if l > 0:
-            bwd_pack_send(l - 1, 0, lambda k: solr[l, k // OWN, pl.ds(k % OWN, 1)])
-        emit(l)
+    finish_wait(0)
+    emit(0)
 
 
 def tables(parent_owner, parent_local, ncol):
@@ -451,20 +528,25 @@
             pltpu.VMEM((LEVELS, NR, OWN, 16, 128), F32),
             pltpu.VMEM((LEVELS, OWN, 128, 256), BF16),
             pltpu.VMEM((LEVELS, OWN, 128, 256), BF16),
+            pltpu.VMEM((3, NR, OWN, 16, 128), F32),
+            pltpu.VMEM((3, OWN, 128, 256), BF16),
             pltpu.VMEM((LEVELS, NR, OWN) + tile, F32),
             pltpu.VMEM((LEVELS, NR, OWN) + tile, F32),
-            pltpu.VMEM((LEVELS, NR, OWN, 64, 128), F32),
+            pltpu.VMEM((3, NR, OWN) + tile, F32),
+            pltpu.VMEM((3, NR, OWN) + tile, F32),
+            pltpu.VMEM((LEVELS, OWN, 64, 128), F32),
+            pltpu.VMEM((2, NR, OWN, 64, 128), F32),
             pltpu.VMEM((SUP, ANC) + tile, F32),
             pltpu.VMEM((SUP, ANC) + tile, F32),
             pltpu.VMEM((SLOTS + 1, 6) + tile, F32),
             fsend, frecv, pltpu.VMEM((3, 3, SLOTS, 1) + tile, F32), pltpu.VMEM((SLOTS, 7) + tile, F32), bbuf,
             pltpu.VMEM((3, SUP, ANC) + tile, F32),
-            pltpu.VMEM((NR, OWN, 64, 128), F32),
+            pltpu.VMEM((2, NR, OWN, 64, 128), F32),
             pltpu.VMEM((2, 2, 4, OWN, 64, 128), F32),
             pltpu.VMEM((OWN, 64, 128), F32),
             pltpu.VMEM((LEVELS, NR, OWN) + tile, F32),
             pltpu.VMEM((LEVELS, NR, OWN) + tile, F32),
-            sems((2,)), sems((3, LEVELS)), sems((2, LEVELS, 2)),
+            sems((2,)), sems((3, LEVELS)), sems((3, 3)), sems((2, 3)), sems((2, LEVELS, 2)),
             sems((LEVELS, OWN, 4, 2)), sems((LEVELS, OWN, 4, 2)),
             sems((3, 3)), sems((3, 3)), sems((3, 4)), sems((3, 4)),
             sems((LEVELS, OWN, 4, 2)), sems((LEVELS, OWN, 4, 2)), sems((2, LEVELS, 2)),

time: 286 us -> 277 us (0.969)
  Pallas kernels: 257 us -> 248 us
    pallas_call x1, Pallas kernels: 257 us -> 248 us  [per_device(): pl.pallas_call(functools.partial(kernel, ncol), out_shape=(jax.ShapeDtype...]
where the time goes in v3:
time: 277 us; the launch traced here: 275 us
  Pallas kernels  248 us (90%)
  local copies, waits for them, and re-layouts  16.9 us (6%)
  starting transfers between devices  7.62 us (3%)
    pallas_call x1, Pallas kernels, per_device(): pl.pallas_call(functools.partial(kernel, ncol), out_shape=(jax.ShapeDtype...  248 us
    all_to_all x1, starting transfers between devices, tables(): lax.all_to_all(ids.reshape(3, ncol, cap), 'col', split_axis=1, concat_axi...  7.62 us
  transfers between devices with their start and end apart: 1, of which 0 were waited for; matrix products, arithmetic and copies ran while one was open for 3% of the time, Pallas kernels for 0%

profile of v3, /device:TPU:2, one launch (start us, length us, event | category | flops | bytes accessed | tf_op | source)
XLA Modules:
  0.0 274.9 jit_solution(10366750153238313156)
XLA Ops:
  0.6 0.7 copy.58
  1.3 0.1 convert_reduce_fusion
  1.4 0.7 multiply_add_fusion
  2.1 0.1 select_reduce_fusion.2
  2.2 0.7 copy.48
  2.9 7.6 %all-to-all-start = ((s32[3,32,2]{0,2,1:T(2,128)}), s32[3,32,2]{0,2,1:T(2,128)S(1)}, u32[]{:S(2)}, u32[]{:S(2)}) async-start(s32[3,32,2]{0,2,1:T(2,128)} %bitcast), calls=%async_computation | async-start | bytes 65536 | tf_op jit(solution)/shard_map/all_to_all | solution.py:492
  10.6 3.2 %copy.56 = f32[2,8,32,8,64]{4,0,1,3,2:T(2,128)S(1)} copy(f32[2,8,32,8,64]{4,3,2,1,0:T(8,128)} %bitcast.27) | data formatting | bytes 2097152 | tf_op jit(solution)/shard_map/reshape | solution.py:507
  13.8 0.0 copy-start
  13.9 2.1 reshape.108.anc
  16.0 0.0 copy-start.2
  16.0 0.0 copy-done
  16.0 0.8 copy.57
  16.8 1.4 reshape.106.rhs
  18.2 0.0 copy-done.2
  18.2 0.6 copy.45.pat
  18.8 0.0 all-to-all-done
  18.8 0.1 copy.49
  18.9 0.2 select_reduce_fusion
  19.1 0.2 select_reduce_fusion.1
  19.4 0.1 copy.40
  19.5 0.1 copy.41
  19.6 0.1 max.15
  19.7 0.6 stack.17.tab
  20.3 248.1 %shard_map.86 = (f32[4,32,8,128]{3,2,1,0:T(8,128)}, f32[32,8,8,128]{3,2,1,0:T(8,128)}) custom-call(s32[3,5,64]{2,1,0:T(8,128)} %stack.17.tab, s32[4,7,32]{2,1,0:T(8,128)} %copy.45.pat, f32[4,32,8,128]{3,2,1,0:T(8,128)} %reshape.106.rhs, f32[32,8,8,128]{3,2,1,0:T(8,128)} %reshape.108.anc, f32[4,32,16,128]{3,2,1,0:T(8,128)} %dinv.1, f32[4,8,32,16,128]{4,3,2,1,0:T(8,128)} %panels.1), custom_call_target="tpu_custom_call" | custom-call | flops 4000000000 | bytes 12000000 | tf_op jit(solution)/shard_map/pallas_call | solution.py:516
  268.5 2.5 reshape.111
  271.0 0.0 copy-start.1
  271.0 2.0 copy.47
  272.9 0.0 copy-done.1
  272.9 0.6 reshape.109
  273.6 1.3 copy.46
  (11 shorter events, 0.1 us)
Async XLA Ops:
  2.9 15.9 %all-to-all-start = ((s32[3,32,2]{0,2,1:T(2,128)}), s32[3,32,2]{0,2,1:T(2,128)S(1)}, u32[]{:S(2)}, u32[]{:S(2)}) async-start(s32[3,32,2]{0,2,1:T(2,128)} %bitcast), calls=%async_computation | async-start | bytes 65536 | tf_op jit(solution)/shard_map/all_to_all | solution.py:492
  13.8 2.1 copy-start
  16.0 2.2 copy-start.2
  271.0 2.0 copy-start.1

commit v4 on v3

--- a/solution.py
+++ b/solution.py
@@ -15,8 +15,12 @@
 SLOTS = 64
 NR = 8
 OWN = SUP // NR
-FWD_GROUPS = ((0, 1), (1, 2), (2, 8))
-BWD_GROUPS = (((0, 1), (1, 2), (2, 3), (3, 8)), ((0, 1), (1, 2), (2, 8)), ((0, 1), (1, 8)))
+FWD_GROUPS = ((0, 1), (1, 2), (2, 3), (3, 4), (4, 6), (6, 8))
+BWD_GROUPS = (
+    ((0, 1), (1, 2), (2, 3), (3, 5), (5, 7), (7, 8)),
+    ((0, 1), (1, 2), (2, 4), (4, 6), (6, 8)),
+    ((0, 1), (1, 8)),
+)
 FSRC, POS, PREV, LAST, BSRC = range(5)
 
 
@@ -86,6 +90,16 @@
     load_panels(3).start()
     pl.semaphore_wait(barrier, NR - 1 + ncol - 1)
 
+    def out_at(l, g, a, b):
+        if l < 2:
+            return out.at[l, g, pl.ds(a, b - a)]
+        return stage.at[0, pl.ds(a, b - a), g, pl.ds(8 * (l - 2), 8)]
+
+    def car_at(l, g, a, b):
+        if l == 1:
+            return car.at[g, pl.ds(a, b - a)]
+        return stage.at[1, pl.ds(a, b - a), g, pl.ds(8 * (l - 2), 8)]
+
     def row_send(src, dst, send_sem, recv_sem):
         for k in (4, 3, 5, 2, 6, 1, 7):
             z = lax.rem(row + k, NR)
@@ -155,8 +169,7 @@
             pack(src, dst, col * cap + i)
         dst[pl.ds(col * cap, cap)] = src[pl.ds(col * cap, cap)]
 
-        def one(k):
-            c = lax.rem(col + k, ncol)
+        def one(c):
             for i in range(cap):
                 pack(src, dst, c * cap + i)
             pltpu.make_async_remote_copy(
@@ -165,14 +178,19 @@
                 device_id={"col": c}, device_id_type=pl.DeviceIdType.MESH,
             ).start()
 
-        steps = (ncol - 1) // 3
-
-        @pl.loop(0, steps)
-        def _(k):
-            for i in range(3):
-                one(3 * k + i + 1)
-        for k in range(3 * steps + 1, ncol):
-            one(k)
+        if ncol == 32:
+            x, y, core = col // 8, lax.rem(col // 2, 4), lax.rem(col, 2)
+
+            @pl.loop(1, 16, unroll=3)
+            def _(k):
+                chip = lax.rem(x + k, 4) * 8 + lax.rem(y + k + k // 4, 4) * 2
+                one(chip + core)
+                one(chip + 1 - core)
+            one(col + 1 - 2 * core)
+        else:
+            @pl.loop(1, ncol)
+            def _(k):
+                one(lax.rem(col + k, ncol))
 
     def col_wait(dst, sem):
         wait_bytes(dst.at[pl.ds(0, SLOTS - cap)], sem)
@@ -184,9 +202,9 @@
         def pack(src, dst, s):
             k = tab[l, FSRC, s]
             if l == 0:
-                src[s] = out[k, pl.ds(a, b - a)]
+                src[s] = out_at(l, k, a, b)[...]
             else:
-                src[s] = out[k, pl.ds(a, b - a)] + car[k, pl.ds(a, b - a)]
+                src[s] = out_at(l, k, a, b)[...] + car_at(l, k, a, b)[...]
         col_send(src, dst, sem_fs.at[l, g], sem_fr.at[l, g], pack)
 
     def fwd_collect(l, g):
@@ -206,11 +224,13 @@
         else:
             @pl.loop(0, SUP, unroll=4)
             def _(p):
-                car[p, pl.ds(a - 1, b - a)] = cum[tab[l, LAST, p], pl.ds(0, b - a)]
+                car_at(l + 1, p, a - 1, b - 1)[...] = cum[tab[l, LAST, p], pl.ds(0, b - a)]
 
     def bwd_buffer(l, g):
         a, b = BWD_GROUPS[l][g]
-        return bulk.at[:, pl.ds(0, b - a)] if b - a > 1 else bsend.at[l, g]
+        if b - a == 1 and g < 3:
+            return bsend.at[l, g]
+        return bulk.at[:, pl.ds(a - (3, 2, 1)[l], b - a)]
 
     def bwd_pack_send(l, g, source):
         src, dst = bwd_buffer(l, g), brecv[l][g]
@@ -257,7 +277,7 @@
         return (0, 1) if t < 4 else (c % 2,)
 
     def product(l, g):
-        out[g] = multiply(ph[l, g], sol[l % 2, g // OWN, g % OWN].reshape(8, 8, 128))
+        out_at(l, g, 0, 8)[...] = multiply(ph[l, g], sol[l % 2, g // OWN, g % OWN].reshape(8, 8, 128))
 
     def solve(l):
         for c in range(OWN):
@@ -370,20 +390,24 @@
                 convert(2, 16 * t, 16 * t + 16)
             elif t == 2:
                 ring_step(3, 2)
-                bwd_gather(2, 1)
-                bwd_pack_send(1, 2, lambda k: anct[2, k, pl.ds(1, 6)])
+                fwd_collect(0, 1)
             else:
-                fwd_collect(0, 1)
                 fwd_collect(0, 2)
+
+                @pl.loop(0, SUP)
+                def _(g):
+                    car_at(2, g, 7, 8)[...] = jnp.zeros((1, 8, 128), F32)
         else:
             if t < 2:
                 partial_sums(2, 16 * t, 16 * t + 16)
             elif t == 2:
-                bwd_gather(1, 2)
-                bwd_pack_send(0, 3, lambda k: anct[1, k, pl.ds(2, 5)])
+                fwd_collect(1, 1)
             else:
-                fwd_collect(1, 1)
                 fwd_collect(1, 2)
+
+    def relay(l, g):
+        a, b = BWD_GROUPS[l][g]
+        bwd_pack_send(l, g, lambda k: anct[l + 1, k, pl.ds(a - 1, b - a)])
 
     rsend[0] = rhs[0].reshape(NR, OWN, 8, 128)
     r_send(0)
@@ -409,18 +433,36 @@
         fwd_collect(l, 0)
         r_send(l + 1)
         p0_send(l)
-        fwd_pack_send(l, 2)
+        if l == 0:
+            fwd_pack_send(0, 2)
+            fwd_pack_send(0, 3)
+            bwd_gather(2, 1)
+            relay(1, 2)
+            fwd_pack_send(0, 4)
+        if l == 1:
+            fwd_collect(0, 3)
+            fwd_pack_send(1, 2)
+            fwd_collect(0, 4)
+            fwd_pack_send(1, 3)
+            relay(1, 3)
+            relay(1, 4)
+        if l == 2:
+            bwd_gather(1, 2)
+            relay(0, 3)
         dinv_wait(l + 1)
 
     ring_step(2, 1)
     ring_end(3)
     solve(3)
     finish_all(3)
+    bwd_gather(1, 3)
+    relay(0, 4)
     ring_step(2, 2)
     ring_step(2, 3)
     p0_wait(2)
     finish_wait(3)
     send_down(2)
+    fwd_pack_send(0, 5)
     spread_step(3, 0)
     ring_step(2, 4)
     p0_wait(1)
@@ -429,35 +471,49 @@
 
     a_send(2)
     bwd_pack_send(1, 1, lambda k: asend[2, k // OWN, pl.ds(k % OWN, 1)])
+    bwd_gather(1, 4)
+    relay(0, 5)
     ring_end(2)
     spread_step(3, 2)
     a_wait(2)
     finish_all(2)
     p0_wait(0)
+    fwd_collect(0, 5)
+    fwd_pack_send(1, 4)
     bwd_gather(1, 1)
     partial_sums(1, 0, SUP)
     ring_step(1, 1)
     finish_wait(2)
     send_down(1)
+    fwd_pack_send(1, 5)
     ring_step(1, 2)
     emit(2)
     ring_step(1, 3)
 
     a_send(1)
     bwd_pack_send(0, 1, lambda k: asend[1, k // OWN, pl.ds(k % OWN, 1)])
-    bwd_pack_send(0, 2, lambda k: anct[1, k, pl.ds(1, 1)])
+    relay(0, 2)
+    fwd_collect(1, 3)
+    fwd_pack_send(2, 2)
     ring_step(1, 4)
     bwd_gather(0, 3)
+    bwd_gather(0, 4)
     ring_end(1)
     a_wait(1)
     finish_all(1)
+    bwd_gather(0, 5)
+    bwd_gather(0, 1)
     bwd_gather(0, 2)
-    bwd_gather(0, 1)
     partial_sums(0, 0, SUP)
     ring_step(0, 1)
     finish_wait(1)
     send_down(0)
+    fwd_collect(1, 4)
+    fwd_pack_send(2, 3)
     ring_step(0, 2)
+    fwd_collect(1, 5)
+    fwd_pack_send(2, 4)
+    fwd_pack_send(2, 5)
     emit(1)
     ring_step(0, 3)
 
@@ -468,13 +524,13 @@
     a_wait(0)
     finish_all(0)
     spread_step(3, 4)
-    fwd_collect(2, 1)
-    fwd_collect(2, 2)
+    for g in range(1, 6):
+        fwd_collect(2, g)
 
     @pl.loop(0, SUP)
     def _(g):
-        bu_out[g, pl.ds(0, 7)] = out[g, pl.ds(0, 7)] + car[g, pl.ds(0, 7)]
-        bu_out[g, 7] = out[g, 7]
+        bu_out[g, pl.ds(0, 7)] = out_at(3, g, 0, 7)[...] + car_at(3, g, 0, 7)[...]
+        bu_out[g, pl.ds(7, 1)] = out_at(3, g, 7, 8)[...]
     finish_wait(0)
     emit(0)
 
@@ -536,9 +592,9 @@
             pltpu.VMEM((3, NR, OWN) + tile, F32),
             pltpu.VMEM((LEVELS, OWN, 64, 128), F32),
             pltpu.VMEM((2, NR, OWN, 64, 128), F32),
+            pltpu.VMEM((2, SUP, ANC) + tile, F32),
             pltpu.VMEM((SUP, ANC) + tile, F32),
-            pltpu.VMEM((SUP, ANC) + tile, F32),
-            pltpu.VMEM((SLOTS + 1, 6) + tile, F32),
+            pltpu.VMEM((SLOTS + 1, 2) + tile, F32),
             fsend, frecv, pltpu.VMEM((3, 3, SLOTS, 1) + tile, F32), pltpu.VMEM((SLOTS, 7) + tile, F32), bbuf,
             pltpu.VMEM((3, SUP, ANC) + tile, F32),
             pltpu.VMEM((2, NR, OWN, 64, 128), F32),
@@ -548,7 +604,7 @@
             pltpu.VMEM((LEVELS, NR, OWN) + tile, F32),
             sems((2,)), sems((3, LEVELS)), sems((3, 3)), sems((2, 3)), sems((2, LEVELS, 2)),
             sems((LEVELS, OWN, 4, 2)), sems((LEVELS, OWN, 4, 2)),
-            sems((3, 3)), sems((3, 3)), sems((3, 4)), sems((3, 4)),
+            sems((3, 6)), sems((3, 6)), sems((3, 6)), sems((3, 6)),
             sems((LEVELS, OWN, 4, 2)), sems((LEVELS, OWN, 4, 2)), sems((2, LEVELS, 2)),
         ],
         compiler_params=pltpu.CompilerParams(

time: 277 us -> 236 us (0.85)
  Pallas kernels: 248 us -> 208 us
    pallas_call x1, Pallas kernels: 248 us -> 208 us  [per_device(): pl.pallas_call(functools.partial(kernel, ncol), out_shape=(jax.ShapeDtype...]
where the time goes in v4:
time: 236 us; the launch traced here: 235 us
  Pallas kernels  208 us (88%)
  local copies, waits for them, and re-layouts  16.9 us (7%)
  starting transfers between devices  7.62 us (3%)
    pallas_call x1, Pallas kernels, per_device(): pl.pallas_call(functools.partial(kernel, ncol), out_shape=(jax.ShapeDtype...  208 us
    all_to_all x1, starting transfers between devices, tables(): lax.all_to_all(ids.reshape(3, ncol, cap), 'col', split_axis=1, concat_axi...  7.62 us
    reshape x2, local copies, waits for them, and re-layouts, per_device(): ancestor_solution.reshape(2, 8, SUP, ANC, 64).transpose(2, 3, 1, 0, 4)  5.34 us
  transfers between devices with their start and end apart: 1, of which 0 were waited for; matrix products, arithmetic and copies ran while one was open for 3% of the time, Pallas kernels for 0%

profile of v4, /device:TPU:2, one launch (start us, length us, event | category | flops | bytes accessed | tf_op | source)
XLA Modules:
  0.0 234.9 jit_solution(1668281714944736843)
XLA Ops:
  0.6 0.7 copy.58
  1.3 0.1 convert_reduce_fusion
  1.4 0.7 multiply_add_fusion
  2.1 0.1 select_reduce_fusion.2
  2.2 0.7 copy.48
  2.9 7.6 %all-to-all-start = ((s32[3,32,2]{0,2,1:T(2,128)}), s32[3,32,2]{0,2,1:T(2,128)S(1)}, u32[]{:S(2)}, u32[]{:S(2)}) async-start(s32[3,32,2]{0,2,1:T(2,128)} %bitcast), calls=%async_computation | async-start | bytes 65536 | tf_op jit(solution)/shard_map/all_to_all | solution.py:548
  10.6 3.2 %copy.56 = f32[2,8,32,8,64]{4,0,1,3,2:T(2,128)S(1)} copy(f32[2,8,32,8,64]{4,3,2,1,0:T(8,128)} %bitcast.27) | data formatting | bytes 2097152 | tf_op jit(solution)/shard_map/reshape | solution.py:563
  13.8 0.0 copy-start
  13.9 2.1 reshape.108.anc
  16.0 0.0 copy-start.2
  16.0 0.0 copy-done
  16.0 0.8 copy.57
  16.8 1.4 reshape.106.rhs
  18.2 0.0 copy-done.2
  18.2 0.6 copy.45.pat
  18.8 0.0 all-to-all-done
  18.8 0.1 copy.49
  18.9 0.2 select_reduce_fusion
  19.1 0.2 select_reduce_fusion.1
  19.4 0.1 copy.40
  19.5 0.1 copy.41
  19.6 0.1 max.15
  19.7 0.6 stack.17.tab
  20.3 208.2 %shard_map.86 = (f32[4,32,8,128]{3,2,1,0:T(8,128)}, f32[32,8,8,128]{3,2,1,0:T(8,128)}) custom-call(s32[3,5,64]{2,1,0:T(8,128)} %stack.17.tab, s32[4,7,32]{2,1,0:T(8,128)} %copy.45.pat, f32[4,32,8,128]{3,2,1,0:T(8,128)} %reshape.106.rhs, f32[32,8,8,128]{3,2,1,0:T(8,128)} %reshape.108.anc, f32[4,32,16,128]{3,2,1,0:T(8,128)} %dinv.1, f32[4,8,32,16,128]{4,3,2,1,0:T(8,128)} %panels.1), custom_call_target="tpu_custom_call" | custom-call | flops 4000000000 | bytes 12000000 | tf_op jit(solution)/shard_map/pallas_call | solution.py:572
  228.5 2.5 %reshape.111 = f32[32,8,8,2,64]{4,3,2,1,0:T(2,128)S(1)} reshape(f32[32,8,8,128]{3,2,1,0:T(8,128)} %get-tuple-element.5) | data formatting | bytes 2097152 | tf_op jit(solution)/shard_map/reshape | solution.py:616
  231.0 0.0 copy-start.1
  231.0 2.0 copy.47
  233.0 0.0 copy-done.1
  233.0 0.6 reshape.109
  233.6 1.3 copy.46
  (11 shorter events, 0.1 us)
Async XLA Ops:
  2.9 15.9 %all-to-all-start = ((s32[3,32,2]{0,2,1:T(2,128)}), s32[3,32,2]{0,2,1:T(2,128)S(1)}, u32[]{:S(2)}, u32[]{:S(2)}) async-start(s32[3,32,2]{0,2,1:T(2,128)} %bitcast), calls=%async_computation | async-start | bytes 65536 | tf_op jit(solution)/shard_map/all_to_all | solution.py:548
  13.8 2.1 copy-start
  16.0 2.2 copy-start.2
  231.0 2.0 copy-start.1

commit v5 on v4

--- a/solution.py
+++ b/solution.py
@@ -21,7 +21,8 @@
     ((0, 1), (1, 2), (2, 4), (4, 6), (6, 8)),
     ((0, 1), (1, 8)),
 )
-FSRC, POS, PREV, LAST, BSRC = range(5)
+FSRC, POS = range(2)
+PREV, LAST, BSRC = range(3)
 
 
 def low_lanes(shape):
@@ -57,10 +58,11 @@
 
 
 def kernel(
-    ncol, tab, pat, rhs, anc, dinv, panels, sol_out, bu_out,
+    ncol, tab, pat, rhs, anc, ids, dinv, panels, sol_out, bu_out,
+    idr, arrv, arr,
     stage, ph, pt, dv, dh, dt, pv, p0, rsend, rs, asend, ar, own, sol, out, car, cum, fsend, frecv, bsend, bulk, brecv, anct,
     part, rsr, tot, xsend, solr,
-    sem_stage, sem_dv, sem_p, sem_a, sem_r, sem_ag_s, sem_ag_r, sem_fs, sem_fr, sem_bs, sem_br, sem_rs_s, sem_rs_r, sem_x,
+    sem_id, sem_stage, sem_dv, sem_p, sem_a, sem_r, sem_ag_s, sem_ag_r, sem_fs, sem_fr, sem_bs, sem_br, sem_rs_s, sem_rs_r, sem_x,
 ):
     row, col = lax.axis_index("row"), lax.axis_index("col")
     cap = SLOTS // ncol
@@ -215,16 +217,16 @@
 
         @pl.loop(0, SLOTS, unroll=4)
         def _(s):
-            cum[s, pl.ds(0, b - a)] = dst[s] + cum[tab[l, PREV, s], pl.ds(0, b - a)]
+            cum[s, pl.ds(0, b - a)] = dst[s] + cum[arr[3 * l + PREV, s], pl.ds(0, b - a)]
 
         if g == 0:
             @pl.loop(0, SUP, unroll=4)
             def _(p):
-                rsend[l + 1, p // OWN, p % OWN] = rhs[l + 1, p] - cum[tab[l, LAST, p], 0]
+                rsend[l + 1, p // OWN, p % OWN] = rhs[l + 1, p] - cum[arr[3 * l + LAST, p], 0]
         else:
             @pl.loop(0, SUP, unroll=4)
             def _(p):
-                car_at(l + 1, p, a - 1, b - 1)[...] = cum[tab[l, LAST, p], pl.ds(0, b - a)]
+                car_at(l + 1, p, a - 1, b - 1)[...] = cum[arr[3 * l + LAST, p], pl.ds(0, b - a)]
 
     def bwd_buffer(l, g):
         a, b = BWD_GROUPS[l][g]
@@ -236,7 +238,7 @@
         src, dst = bwd_buffer(l, g), brecv[l][g]
 
         def pack(src, dst, s):
-            src[s] = source(tab[l, BSRC, s])
+            src[s] = source(arr[3 * l + BSRC, s])
         col_send(src, dst, sem_bs.at[l, g], sem_br.at[l, g], pack)
 
     def bwd_gather(l, g):
@@ -249,12 +251,51 @@
         def _(k):
             anct[l, k, pl.ds(a, b - a)] = dst[tab[l, POS, k]]
 
+    def ids_send():
+        idr[col] = ids[col]
+
+        @pl.loop(1, ncol)
+        def _(k):
+            c = lax.rem(col + k, ncol)
+            pltpu.make_async_remote_copy(
+                src_ref=ids.at[c], dst_ref=idr.at[col], send_sem=sem_id.at[0], recv_sem=sem_id.at[1],
+                device_id={"col": c}, device_id_type=pl.DeviceIdType.MESH,
+            ).start()
+
+    def ids_wait():
+        wait_bytes(idr.at[pl.ds(0, ncol - 1)], sem_id.at[1])
+        wait_bytes(idr.at[pl.ds(0, ncol - 1)], sem_id.at[0])
+        lane = lax.broadcasted_iota(jnp.int32, (8, 128), 1)
+        odd = lax.rem(lax.broadcasted_iota(jnp.int32, (8, 128), 0), 2)
+        mine = lax.rem(lane, 2) == odd
+        zero = jnp.zeros((8, 128), jnp.int32)
+        half = zero
+        for c in range(32):
+            half = half + jnp.where(mine & (lane // 2 == c), idr[c], zero)
+        every = half + jnp.where(odd == 0, pltpu.roll(half, 7, 0), pltpu.roll(half, 1, 0))
+        prev, last = zero - 1, zero - 1
+        for c in range(32):
+            tile, slot = idr[c], odd + 2 * c
+            prev = jnp.maximum(prev, jnp.where((tile == every) & (slot < lane), slot, -1))
+            last = jnp.maximum(last, jnp.where(tile == lane + 1, slot, -1))
+        prev = jnp.maximum(prev, jnp.where(odd == 0, pltpu.roll(prev, 7, 0), pltpu.roll(prev, 1, 0)))
+        last = jnp.maximum(last, jnp.where(odd == 0, pltpu.roll(last, 7, 0), pltpu.roll(last, 1, 0)))
+        prev = jnp.where(prev < 0, SLOTS, prev)
+        last = jnp.where(last < 0, SLOTS, last)
+        source = jnp.maximum(every - 1, 0)
+        for l in range(3):
+            for kind, value in ((PREV, prev), (LAST, last), (BSRC, source)):
+                arrv[3 * l + kind : 3 * l + kind + 1, :] = value[2 * l : 2 * l + 1, :]
+        copy = pltpu.make_async_copy(arrv, arr, sem_id.at[2])
+        copy.start()
+        copy.wait()
+
     def convert(l, low=0, high=SUP):
         place = (0, 0, 1, 1)[l]
         if low == 0:
             load_panels(l).wait()
 
-        @pl.loop(low, high)
+        @pl.loop(low, high, unroll=2)
         def _(g):
             blocks = [stage[place, 0, g]]
             for d in range(1, ANC):
@@ -347,7 +388,7 @@
                     rs_copy(l, c, t, way).wait_send()
 
     def partial_sums(l, low, high):
-        @pl.loop(low, high, unroll=2)
+        @pl.loop(low, high, unroll=4)
         def _(g):
             part[l % 2, g // OWN, g % OWN] = multiply(pt[l, g], anc[g] if l == 3 else anct[l, g]).reshape(64, 128)
 
@@ -413,7 +454,9 @@
     r_send(0)
     dinv_send(0)
     cum[SLOTS] = jnp.zeros(cum.shape[1:], F32)
-    bwd_pack_send(2, 1, lambda k: anc[k, pl.ds(0, 7)])
+    ids_send()
+    for r in range(9, 16):
+        arrv[r : r + 1, :] = jnp.zeros((1, 128), jnp.int32)
 
     @pl.loop(0, SUP)
     def _(g):
@@ -421,6 +464,8 @@
         for l in range(3):
             anct[l, g, 0] = jnp.zeros((8, 128), F32)
     convert(0)
+    ids_wait()
+    bwd_pack_send(2, 1, lambda k: anc[k, pl.ds(0, 7)])
     convert(3)
     dinv_wait(0)
     for l in range(LEVELS - 1):
@@ -458,13 +503,12 @@
     bwd_gather(1, 3)
     relay(0, 4)
     ring_step(2, 2)
-    ring_step(2, 3)
     p0_wait(2)
     finish_wait(3)
     send_down(2)
     fwd_pack_send(0, 5)
+    ring_step(2, 3)
     spread_step(3, 0)
-    ring_step(2, 4)
     p0_wait(1)
     emit(3)
     spread_step(3, 1)
@@ -473,8 +517,9 @@
     bwd_pack_send(1, 1, lambda k: asend[2, k // OWN, pl.ds(k % OWN, 1)])
     bwd_gather(1, 4)
     relay(0, 5)
+    ring_step(2, 4)
+    spread_step(3, 2)
     ring_end(2)
-    spread_step(3, 2)
     a_wait(2)
     finish_all(2)
     p0_wait(0)
@@ -545,20 +590,15 @@
     hit = pos[:, None, :] == slots[None, :, None]
     fsrc = jnp.sum(jnp.where(hit, here[None, None, :], 0), axis=2)
     ids = jnp.sum(jnp.where(hit, parent_local[:, None, :] + 1, 0), axis=2)
-    ids = lax.all_to_all(ids.reshape(3, ncol, cap), "col", split_axis=1, concat_axis=1, tiled=True).reshape(3, SLOTS)
-    equal = (ids[:, :, None] == ids[:, None, :]) & (slots[None, None, :] < slots[None, :, None])
-    prev = jnp.max(jnp.where(equal, slots[None, None, :], -1), axis=2)
-    prev = jnp.where(prev < 0, SLOTS, prev)
-    mine = ids[:, None, :] == here[None, :, None] + 1
-    last = jnp.max(jnp.where(mine, slots[None, None, :], -1), axis=2)
-    last = jnp.where(last < 0, SLOTS, last)
-    bsrc = jnp.maximum(ids - 1, 0)
+    ids = ids.reshape(3, ncol, cap).transpose(1, 0, 2).reshape(ncol, 3 * cap)
+    ids = jnp.pad(ids, ((0, 0), (0, 8 - 3 * cap)))
+    ids = jnp.broadcast_to(ids[:, :, None], (ncol, 8, 128))
     wide = lambda x: jnp.pad(x, ((0, 0), (0, SLOTS - x.shape[1])))
-    return jnp.stack([fsrc, wide(pos), prev, wide(last), bsrc], axis=1)
+    return jnp.stack([fsrc, wide(pos)], axis=1), ids
 
 
 def per_device(ncol, rhs, dinv, panels, pattern, parent_owner, parent_local, ancestor_solution):
-    tab = tables(parent_owner, parent_local, ncol)
+    tab, ids = tables(parent_owner, parent_local, ncol)
     rhs_p = rhs.reshape(LEVELS, 2, 8, SUP, 64).transpose(0, 3, 2, 1, 4).reshape(LEVELS, SUP, 8, 128)
     anc_p = ancestor_solution.reshape(2, 8, SUP, ANC, 64).transpose(2, 3, 1, 0, 4).reshape(SUP, ANC, 8, 128)
     vmem = pl.BlockSpec(memory_space=pltpu.VMEM)
@@ -575,9 +615,12 @@
             jax.ShapeDtypeStruct((LEVELS, SUP) + tile, F32),
             jax.ShapeDtypeStruct((SUP, ANC) + tile, F32),
         ),
-        in_specs=[smem, smem, vmem, vmem, anywhere, anywhere],
+        in_specs=[smem, smem, vmem, vmem, vmem, anywhere, anywhere],
         out_specs=(vmem, vmem),
         scratch_shapes=[
+            pltpu.VMEM((32,) + tile, jnp.int32),
+            pltpu.VMEM((16, 128), jnp.int32),
+            pltpu.SMEM((16, 128), jnp.int32),
             pltpu.VMEM((2, ANC, SUP, 16, 128), F32),
             pltpu.VMEM((LEVELS, SUP, 128, 256), BF16),
             pltpu.VMEM((LEVELS, SUP, 128, 256), BF16),
@@ -602,7 +645,7 @@
             pltpu.VMEM((OWN, 64, 128), F32),
             pltpu.VMEM((LEVELS, NR, OWN) + tile, F32),
             pltpu.VMEM((LEVELS, NR, OWN) + tile, F32),
-            sems((2,)), sems((3, LEVELS)), sems((3, 3)), sems((2, 3)), sems((2, LEVELS, 2)),
+            sems((3,)), sems((2,)), sems((3, LEVELS)), sems((3, 3)), sems((2, 3)), sems((2, LEVELS, 2)),
             sems((LEVELS, OWN, 4, 2)), sems((LEVELS, OWN, 4, 2)),
             sems((3, 6)), sems((3, 6)), sems((3, 6)), sems((3, 6)),
             sems((LEVELS, OWN, 4, 2)), sems((LEVELS, OWN, 4, 2)), sems((2, LEVELS, 2)),
@@ -611,7 +654,7 @@
             collective_id=0, has_side_effects=True, vmem_limit_bytes=60 * 1024 * 1024
         ),
         cost_estimate=pl.CostEstimate(flops=4 * 10**9, bytes_accessed=12 * 10**6, transcendentals=0),
-    )(tab, pattern, rhs_p, anc_p, dinv, panels)
+    )(tab, pattern, rhs_p, anc_p, ids, dinv, panels)
     solution = sol.reshape(LEVELS, SUP, 8, 2, 64).transpose(0, 3, 2, 1, 4).reshape(LEVELS, 16, SUP, 64)
     boundary = bu.reshape(SUP, ANC, 8, 2, 64).transpose(3, 2, 0, 1, 4).reshape(16, SUP, ANC, 64)
     return solution, boundary

time: 236 us -> 227 us (0.962)
  starting transfers between devices: 7.62 us -> 0 us
    all_to_all x1 -> x0, starting transfers between devices: 7.62 us -> none  [tables(): lax.all_to_all(ids.reshape(3, ncol, cap), 'col', split_axis=1, concat_axi...]
  transfers between devices with their start and end apart: 1 -> 0, of which waited for: 0 -> 0; matrix products, arithmetic and copies ran while one was open for 3% -> 0% of each run, Pallas kernels for 0% -> 0%
where the time goes in v5:
time: 227 us
  Pallas kernels  208 us (92%)
  local copies, waits for them, and re-layouts  16.5 us (7%)
    pallas_call x1, Pallas kernels, per_device(): pl.pallas_call(functools.partial(kernel, ncol), out_shape=(jax.ShapeDtype...  208 us
    reshape x2, local copies, waits for them, and re-layouts, per_device(): ancestor_solution.reshape(2, 8, SUP, ANC, 64).transpose(2, 3, 1, 0, 4)  5.34 us

profile of v5, /device:TPU:2, one launch (start us, length us, event | category | flops | bytes accessed | tf_op | source)
XLA Modules:
  0.0 226.6 jit_solution(6173578617734564387)
XLA Ops:
  0.6 0.7 copy.37
  1.3 0.1 convert_reduce_fusion
  1.4 0.7 multiply_add_fusion
  2.1 0.1 select_reduce_fusion
  2.3 0.6 pad_add_fusion.tab
  2.9 0.1 reshape.65
  3.0 0.1 copy.23
  3.1 0.1 copy.29
  3.2 0.8 broadcast_in_dim.37.ids
  3.9 3.2 %copy.35 = f32[2,8,32,8,64]{4,0,1,3,2:T(2,128)S(1)} copy(f32[2,8,32,8,64]{4,3,2,1,0:T(8,128)} %bitcast.28) | data formatting | bytes 2097152 | tf_op jit(solution)/shard_map/reshape | solution.py:603
  7.1 0.0 copy-start
  7.2 2.1 reshape.64.anc
  9.3 0.0 copy-start.2
  9.3 0.0 copy-done
  9.3 0.8 copy.36
  10.1 1.4 reshape.62.rhs
  11.5 0.0 copy-done.2
  11.5 0.6 copy.25.pat
  12.1 207.9 %shard_map.86 = (f32[4,32,8,128]{3,2,1,0:T(8,128)}, f32[32,8,8,128]{3,2,1,0:T(8,128)}) custom-call(s32[3,2,64]{2,1,0:T(2,128)} %pad_add_fusion.tab, s32[4,7,32]{2,1,0:T(8,128)} %copy.25.pat, f32[4,32,8,128]{3,2,1,0:T(8,128)} %reshape.62.rhs, f32[32,8,8,128]{3,2,1,0:T(8,128)} %reshape.64.anc, s32[32,8,128]{2,1,0:T(8,128)} %broadcast_in_dim.37.ids, ...), custom_call_target="tpu_custom_call" | custom-call | flops 4000000000 | bytes 12000000 | tf_op jit(solution)/shard_map/pallas_call | solution.py:612
  220.0 2.8 %reshape.69 = f32[32,8,8,2,64]{4,3,2,1,0:T(2,128)S(1)} reshape(f32[32,8,8,128]{3,2,1,0:T(8,128)} %get-tuple-element.5) | data formatting | bytes 2097152 | tf_op jit(solution)/shard_map/reshape | solution.py:659
  222.8 0.0 copy-start.1
  222.8 2.0 copy.27
  224.7 0.0 copy-done.1
  224.7 0.6 reshape.67
  225.3 1.3 copy.26
  (6 shorter events, 0.0 us)
Async XLA Ops:
  7.1 2.1 copy-start
  9.3 2.2 copy-start.2
  222.8 2.0 copy-start.1

commit v6 on v5

--- a/solution.py
+++ b/solution.py
@@ -58,8 +58,8 @@
 
 
 def kernel(
-    ncol, tab, pat, rhs, anc, ids, dinv, panels, sol_out, bu_out,
-    idr, arrv, arr,
+    ncol, tab, pat, ids, rhs_whole, anc_whole, dinv, panels, sol_out, bu_out,
+    rhs, anc, rhs_near, anc_near, sem_near, idr, arrv, arr,
     stage, ph, pt, dv, dh, dt, pv, p0, rsend, rs, asend, ar, own, sol, out, car, cum, fsend, frecv, bsend, bulk, brecv, anct,
     part, rsr, tot, xsend, solr,
     sem_id, sem_stage, sem_dv, sem_p, sem_a, sem_r, sem_ag_s, sem_ag_r, sem_fs, sem_fr, sem_bs, sem_br, sem_rs_s, sem_rs_r, sem_x,
@@ -88,6 +88,34 @@
         place = (0, 0, 1, 1)[l]
         return pltpu.make_async_copy(panels.at[l], stage.at[place], sem_stage.at[place])
 
+    def load_rhs(l):
+        return pltpu.make_async_copy(rhs_whole.at[l], rhs_near.at[l % 2], sem_near.at[0, l % 2])
+
+    def load_anc(b):
+        return pltpu.make_async_copy(anc_whole.at[:, pl.ds(8 * b, 8)], anc_near.at[b % 2], sem_near.at[1, b % 2])
+
+    def pack_rows(x):
+        return jnp.swapaxes(jnp.concatenate([x[:8], x[8:]], axis=2), 0, 1)
+
+    def pack_rhs(l):
+        load_rhs(l).wait()
+        for b in range(SUP // 8):
+            rhs[l, 8 * b : 8 * b + 8] = pack_rows(rhs_near[l % 2, :, 8 * b : 8 * b + 8])
+        if l + 2 < LEVELS:
+            load_rhs(l + 2).start()
+
+    def pack_anc(b):
+        load_anc(b).wait()
+
+        @pl.loop(0, 8, unroll=2)
+        def _(g):
+            anc[8 * b + g] = pack_rows(anc_near[b % 2, :, g])
+        if b + 2 < SUP // 8:
+            load_anc(b + 2).start()
+
+    for k in range(2):
+        load_rhs(k).start()
+        load_anc(k).start()
     load_panels(0).start()
     load_panels(3).start()
     pl.semaphore_wait(barrier, NR - 1 + ncol - 1)
@@ -450,6 +478,7 @@
         a, b = BWD_GROUPS[l][g]
         bwd_pack_send(l, g, lambda k: anct[l + 1, k, pl.ds(a - 1, b - a)])
 
+    pack_rhs(0)
     rsend[0] = rhs[0].reshape(NR, OWN, 8, 128)
     r_send(0)
     dinv_send(0)
@@ -463,10 +492,14 @@
         car[g, 7] = jnp.zeros((8, 128), F32)
         for l in range(3):
             anct[l, g, 0] = jnp.zeros((8, 128), F32)
-    convert(0)
+    for b in range(SUP // 8):
+        pack_anc(b)
     ids_wait()
     bwd_pack_send(2, 1, lambda k: anc[k, pl.ds(0, 7)])
+    convert(0)
     convert(3)
+    for l in range(1, LEVELS):
+        pack_rhs(l)
     dinv_wait(0)
     for l in range(LEVELS - 1):
         solve(l)
@@ -599,8 +632,6 @@
 
 def per_device(ncol, rhs, dinv, panels, pattern, parent_owner, parent_local, ancestor_solution):
     tab, ids = tables(parent_owner, parent_local, ncol)
-    rhs_p = rhs.reshape(LEVELS, 2, 8, SUP, 64).transpose(0, 3, 2, 1, 4).reshape(LEVELS, SUP, 8, 128)
-    anc_p = ancestor_solution.reshape(2, 8, SUP, ANC, 64).transpose(2, 3, 1, 0, 4).reshape(SUP, ANC, 8, 128)
     vmem = pl.BlockSpec(memory_space=pltpu.VMEM)
     smem = pl.BlockSpec(memory_space=pltpu.SMEM)
     anywhere = pl.BlockSpec(memory_space=pl.ANY)
@@ -615,9 +646,14 @@
             jax.ShapeDtypeStruct((LEVELS, SUP) + tile, F32),
             jax.ShapeDtypeStruct((SUP, ANC) + tile, F32),
         ),
-        in_specs=[smem, smem, vmem, vmem, vmem, anywhere, anywhere],
+        in_specs=[smem, smem, vmem, anywhere, anywhere, anywhere, anywhere],
         out_specs=(vmem, vmem),
         scratch_shapes=[
+            pltpu.VMEM((LEVELS, SUP) + tile, F32),
+            pltpu.VMEM((SUP, ANC) + tile, F32),
+            pltpu.VMEM((2, 16, SUP, 64), F32),
+            pltpu.VMEM((2, 16, 8, ANC, 64), F32),
+            sems((2, 2)),
             pltpu.VMEM((32,) + tile, jnp.int32),
             pltpu.VMEM((16, 128), jnp.int32),
             pltpu.SMEM((16, 128), jnp.int32),
@@ -651,10 +687,10 @@
             sems((LEVELS, OWN, 4, 2)), sems((LEVELS, OWN, 4, 2)), sems((2, LEVELS, 2)),
         ],
         compiler_params=pltpu.CompilerParams(
-            collective_id=0, has_side_effects=True, vmem_limit_bytes=60 * 1024 * 1024
+            collective_id=0, has_side_effects=True, vmem_limit_bytes=62 * 1024 * 1024
         ),
         cost_estimate=pl.CostEstimate(flops=4 * 10**9, bytes_accessed=12 * 10**6, transcendentals=0),
-    )(tab, pattern, rhs_p, anc_p, ids, dinv, panels)
+    )(tab, pattern, ids, rhs, ancestor_solution, dinv, panels)
     solution = sol.reshape(LEVELS, SUP, 8, 2, 64).transpose(0, 3, 2, 1, 4).reshape(LEVELS, 16, SUP, 64)
     boundary = bu.reshape(SUP, ANC, 8, 2, 64).transpose(3, 2, 0, 1, 4).reshape(16, SUP, ANC, 64)
     return solution, boundary

time: 227 us -> 220 us (0.969)
  local copies, waits for them, and re-layouts: 16.5 us -> 9.66 us
    reshape x4 -> x0, local copies, waits for them, and re-layouts: 7.54 us -> none  [the longest x2 5.34 us: per_device(): ancestor_solution.reshape(2, 8, SUP, ANC, 64).transpose(2, 3, 1, 0, 4)]
where the time goes in v6:
time: 220 us
  Pallas kernels  208 us (95%)
  local copies, waits for them, and re-layouts  9.66 us (4%)
    pallas_call x1, Pallas kernels, per_device(): pl.pallas_call(functools.partial(kernel, ncol), out_shape=(jax.ShapeDtype...  208 us

profile of v6, /device:TPU:2, one launch (start us, length us, event | category | flops | bytes accessed | tf_op | source)
XLA Modules:
  0.0 219.5 jit_solution(10224095029216194290)
XLA Ops:
  0.6 0.7 copy.27
  1.3 0.1 convert_reduce_fusion
  1.4 0.7 multiply_add_fusion
  2.1 0.1 select_reduce_fusion
  2.3 0.6 pad_add_fusion.tab
  2.9 0.1 reshape.49
  3.0 0.1 copy.17
  3.1 0.1 copy.23
  3.2 0.8 broadcast_in_dim.37.ids
  3.9 1.3 copy.19.pat
  5.3 207.7 %shard_map.86 = (f32[4,32,8,128]{3,2,1,0:T(8,128)}, f32[32,8,8,128]{3,2,1,0:T(8,128)}) custom-call(s32[3,2,64]{2,1,0:T(2,128)} %pad_add_fusion.tab, s32[4,7,32]{2,1,0:T(8,128)} %copy.19.pat, s32[32,8,128]{2,1,0:T(8,128)} %broadcast_in_dim.37.ids, f32[4,16,32,64]{3,2,1,0:T(8,128)} %rhs_whole.1, f32[16,32,8,64]{3,2,1,0:T(8,128)} %anc_whole.1, ...), custom_call_target="tpu_custom_call" | custom-call | flops 4000000000 | bytes 12000000 | tf_op jit(solution)/shard_map/pallas_call | solution.py:643
  212.9 2.7 %reshape.53 = f32[32,8,8,2,64]{4,3,2,1,0:T(2,128)S(1)} reshape(f32[32,8,8,128]{3,2,1,0:T(8,128)} %get-tuple-element.5) | data formatting | bytes 2097152 | tf_op jit(solution)/shard_map/reshape | solution.py:695
  215.6 0.0 copy-start
  215.7 2.0 copy.21
  217.6 0.0 copy-done
  217.6 0.6 reshape.51
  218.2 1.3 copy.20
  (6 shorter events, 0.0 us)
Async XLA Ops:
  215.6 2.0 copy-start
